TPU v7x, 512 devices: a whole 4x4x16 slice. The times are simulated.
512 devices in a mesh: lm: 16 (over z), prow: 4 (over y_lo, core), pcol: 8 (over x, y_hi).
Axes of the slice: x: 4, y: 4 (y_hi: 2, y_lo: 2; y = y_hi * 2 + y_lo), z: 16, core: 2. Of those that a mesh axis runs over, the one named last changes fastest.
Arguments:
- queries: bfloat16 [2048, 4096], P('lm', ('prow', 'pcol')), may hold values from -8 to 8
- keys: bfloat16 [2048, 4096], P('lm', ('prow', 'pcol')), may hold values from -6 to 6
- values: bfloat16 [2048, 4096], P('lm', ('prow', 'pcol')), may hold values from -8 to 8
- residual: bfloat16 [2048, 5120], P('lm', ('prow', 'pcol')), may hold values from -2 to 2
- out_proj: bfloat16 [4096, 5120], P(('prow', 'pcol')), may hold values from -0.1875 to 0.1875
- pair_proj: bfloat16 [5120, 256], P(('prow', 'pcol')), may hold values from -0.078125 to 0.078125
- chain_bias: float32 [2, 128], replicated, may hold values from -4 to 4
- ln_gain: float32 [128], replicated, may hold values from 0.1 to 1.9
- w_in: bfloat16 [128, 512], replicated, may hold values from -0.5 to 0.5
- w_out: bfloat16 [512, 128], replicated, may hold values from -0.25 to 0.25
- pair_cot: bfloat16 [1024, 2048, 128], P(('lm', 'prow'), 'pcol'), may hold values from -6 to 6
- residue_mask: int32 [2048], replicated, may hold values from 0 to 1, as said below
- chain_ids: int32 [2048], replicated, may hold values from 0 to 7, never falling along the last dimension, each value on 1 to 1024 neighbouring positions
- slab_start: int32 [1], replicated, may hold values from 0 to 1024
Outputs:
- pair_out: bfloat16 [1024, 2048, 128], P(('lm', 'prow'), 'pcol')
- lm_grad: bfloat16 [2048, 5120], P('lm', ('prow', 'pcol'))
Inputs may be any that keep to these rules, and one draw needn't show every extreme that they name: `residue_mask`: residue 0 is always a residue.
All inputs are finite; a program needn't handle non-finite values.
Results may differ from a plain program's by a relative error of at most 0.035.
Values may be sent and summed in bfloat16 or wider, within the bound.
A program may use at most 64 MiB of HBM per device.

v0:
```python
import math

import jax
import jax.numpy as jnp
from jax import lax
from jax.sharding import PartitionSpec as P

E = 128


def pair_terms(
    a_rows,
    b_columns,
    live_rows,
    live_columns,
    chain_rows,
    chain_columns,
    chain_bias,
    ln_gain,
    w_in,
    w_out,
    pair_cot,
):
    row_count = a_rows.shape[0]
    column_count = b_columns.shape[0]
    width = a_rows.shape[1]
    a_float = a_rows.astype(jnp.float32)
    b_float = b_columns.astype(jnp.float32)
    live_pair = live_rows[:, None] * live_columns[None, :]
    same_chain = chain_rows[:, None] == chain_columns[None, :]
    bias = jnp.where(
        same_chain[:, :, None], chain_bias[1][None, None, :], chain_bias[0][None, None, :]
    )
    pair_seed = live_pair[:, :, None] * (a_float[:, None, :] * b_float[None, :, :] + bias)
    centre = pair_seed - jnp.mean(pair_seed, axis=2, keepdims=True)
    inverse = lax.rsqrt(jnp.mean(centre * centre, axis=2, keepdims=True) + 1e-05)
    normed = centre * inverse
    scaled = (
        (normed * ln_gain[None, None, :])
        .astype(jnp.bfloat16)
        .reshape(row_count * column_count, width)
    )
    hidden = jnp.dot(scaled, w_in, preferred_element_type=jnp.float32)
    sigmoid = jax.nn.sigmoid(hidden)
    act = (hidden * sigmoid).astype(jnp.bfloat16)
    result = pair_seed + jnp.dot(act, w_out, preferred_element_type=jnp.float32).reshape(
        row_count, column_count, width
    )
    flat_cot = pair_cot.reshape(row_count * column_count, width)
    d_act = lax.dot_general(
        flat_cot, w_out, (((1,), (1,)), ((), ())), preferred_element_type=jnp.float32
    )
    d_hidden = (d_act * sigmoid * (1.0 + hidden * (1.0 - sigmoid))).astype(jnp.bfloat16)
    d_scaled = lax.dot_general(
        d_hidden, w_in, (((1,), (1,)), ((), ())), preferred_element_type=jnp.float32
    )
    d_normed = d_scaled.reshape(row_count, column_count, width) * ln_gain[None, None, :]
    d_seed = pair_cot.astype(jnp.float32) + inverse * (
        d_normed
        - jnp.mean(d_normed, axis=2, keepdims=True)
        - normed * jnp.mean(d_normed * normed, axis=2, keepdims=True)
    )
    d_prod = d_seed * live_pair[:, :, None]
    grad_rows = jnp.sum(d_prod * b_float[None, :, :], axis=1)
    grad_columns = jnp.sum(d_prod * a_float[:, None, :], axis=0)
    return (result.astype(jnp.bfloat16), grad_rows, grad_columns)


def body(
    queries,
    keys,
    values,
    residual,
    out_proj,
    pair_proj,
    chain_bias,
    ln_gain,
    w_in,
    w_out,
    pair_cot,
    residue_mask,
    chain_ids,
    slab_start,
):
    row_count = queries.shape[0]
    head_count = queries.shape[1] // E
    scale = 1.0 / math.sqrt(E)
    live = residue_mask.astype(jnp.float32)
    query_split = queries.reshape(row_count, head_count, E)
    highest = jnp.full((head_count, row_count), -1e30, jnp.float32)
    summed = jnp.zeros((row_count, head_count, E), jnp.float32)
    key_piece = lax.all_gather(keys, "lm", axis=0, tiled=True)
    value_piece = lax.all_gather(values, "lm", axis=0, tiled=True)
    length = key_piece.shape[0]
    scores = (
        jnp.einsum(
            "rhe,nhe->hrn",
            query_split,
            key_piece.reshape(length, head_count, E),
            preferred_element_type=jnp.float32,
        )
        * scale
    )
    scores = jnp.where(live[None, None, :] > 0, scores, -1e30)
    newest = jnp.maximum(highest, jnp.max(scores, axis=2))
    factor = jnp.exp(highest - newest)
    shifted = jnp.exp(scores - newest[:, :, None]) * live[None, None, :]
    denominator = jnp.sum(shifted, axis=2)
    weights = shifted.astype(jnp.bfloat16)
    summed = summed * factor.T[:, :, None] + jnp.einsum(
        "hrn,nhe->rhe",
        weights,
        value_piece.reshape(length, head_count, E),
        preferred_element_type=jnp.float32,
    )
    highest, denominator, summed = (newest, denominator, summed)
    attended = (
        (summed / denominator.T[:, :, None]).astype(jnp.bfloat16).reshape(row_count, head_count * E)
    )
    stream_part = lax.psum_scatter(
        lax.dot_general(
            out_proj, attended, (((0,), (1,)), ((), ())), preferred_element_type=jnp.float32
        ).astype(jnp.bfloat16),
        ("prow", "pcol"),
        scatter_dimension=0,
        tiled=True,
    ).astype(jnp.float32)
    stream = (residual.astype(jnp.float32) + stream_part.T).astype(jnp.bfloat16)
    proj_terms = jnp.dot(stream, pair_proj, preferred_element_type=jnp.float32)
    projected_here = lax.psum(proj_terms.astype(jnp.bfloat16), ("prow", "pcol"))
    projected = lax.all_gather(projected_here, "lm", axis=0, tiled=True)
    width = pair_proj.shape[1] // 2
    slab_rows = pair_cot.shape[0]
    column_count = pair_cot.shape[1]
    zero_index = jnp.zeros((), jnp.int32)
    first_row = slab_start[0] + lax.axis_index(("lm", "prow")) * slab_rows
    first_column = lax.axis_index("pcol") * column_count
    a_rows = lax.dynamic_slice(projected, (first_row, zero_index), (slab_rows, width))
    b_columns = lax.dynamic_slice(
        projected, (first_column, zero_index + width), (column_count, width)
    )
    live_rows = lax.dynamic_slice_in_dim(live, first_row, slab_rows)
    live_columns = lax.dynamic_slice_in_dim(live, first_column, column_count)
    chain_rows = lax.dynamic_slice_in_dim(chain_ids, first_row, slab_rows)
    chain_columns = lax.dynamic_slice_in_dim(chain_ids, first_column, column_count)
    pair_out, grad_rows, grad_columns = pair_terms(
        a_rows,
        b_columns,
        live_rows,
        live_columns,
        chain_rows,
        chain_columns,
        chain_bias,
        ln_gain,
        w_in,
        w_out,
        pair_cot,
    )
    total_rows = projected.shape[0]
    local = jnp.zeros((total_rows, 2 * width), jnp.float32)
    local = lax.dynamic_update_slice(local, grad_rows, (first_row, zero_index))
    local = lax.dynamic_update_slice(local, grad_columns, (first_column, zero_index + width))
    summed_all = lax.psum(local, ("lm", "prow", "pcol"))
    owned = lax.dynamic_slice_in_dim(summed_all, lax.axis_index("lm") * row_count, row_count, 0)
    proj_grad = owned.astype(jnp.bfloat16)
    lm_grad = lax.dot_general(
        proj_grad, pair_proj, (((1,), (1,)), ((), ())), preferred_element_type=jnp.float32
    ).astype(jnp.bfloat16)
    return (pair_out, lm_grad)


def solution(mesh):
    return jax.shard_map(
        body,
        mesh=mesh,
        in_specs=(
            P("lm", ("prow", "pcol")),
            P("lm", ("prow", "pcol")),
            P("lm", ("prow", "pcol")),
            P("lm", ("prow", "pcol")),
            P(("prow", "pcol"), None),
            P(("prow", "pcol"), None),
            P(),
            P(),
            P(),
            P(),
            P(("lm", "prow"), "pcol", None),
            P(),
            P(),
            P(),
        ),
        out_specs=(P(("lm", "prow"), "pcol", None), P("lm", ("prow", "pcol"))),
        check_vma=False,
    )
```

profile of v0, /device:TPU:1, one launch (start us, length us, event | category | flops | bytes accessed | tf_op | source)
XLA Modules:
  0.0 581.9 jit_solution(13508212624559094922)
XLA Ops:
  7.2 0.0 copy-start
  7.2 0.0 reduce-scatter.2.cloned.1.call-start
  7.2 0.8 convert_element_type.57
  8.0 0.7 broadcast_compare_fusion.1
  8.7 32.0 %all_gather.9 = bf16[2048,128]{1,0:T(8,128)(2,1)S(1)} all-gather(bf16[128,128]{1,0:T(8,128)(2,1)} %param.15), channel_id=1, replica_groups=mesh['lm'=16,'prow'=4,'pcol'=8] {'lm'}, dimensions={0}, use_global_device_ids=true | all-gather | bytes 557056 | tf_op jit(solution)/shard_map/all_gather | solution.py:92
  40.8 1.1 fusion.29
  41.9 22.2 %all_gather.10 = bf16[2048,128]{1,0:T(8,128)(2,1)S(1)} all-gather(bf16[128,128]{1,0:T(8,128)(2,1)S(1)} %copy-done.12), channel_id=1, replica_groups=mesh['lm'=16,'prow'=4,'pcol'=8] {'lm'}, dimensions={0}, use_global_device_ids=true | all-gather | bytes 557056 | tf_op jit(solution)/shard_map/all_gather | solution.py:93
  64.1 0.3 fusion.12
  64.4 0.0 copy-start.2
  64.4 0.0 copy-start.19
  64.5 2.0 fusion
  66.4 0.0 reduce-scatter.2.cloned.1.call-update
  66.4 0.0 all-reduce.3.cloned.1.call-start
  66.5 158.2 %reduce-scatter.2.cloned.1.call-done = bf16[160,128]{1,0:T(8,128)(2,1)} async-done(((bf16[5120,128]{1,0:T(8,128)(2,1)}), bf16[160,128]{1,0:T(8,128)(2,1)}) %reduce-scatter.2.cloned.1.call-update) | async-done | bytes 40976 | tf_op jit(solution)/shard_map/reduce_scatter | solution.py:120
  224.7 1.6 convolution_convert_fusion.1
  226.4 0.0 all-reduce.3.cloned.1.call-update
  226.4 0.0 all-gather.2.cloned.1.call-start
  226.4 125.9 %all-reduce.3.cloned.1.call-done = bf16[128,256]{1,0:T(8,128)(2,1)} async-done(((bf16[128,256]{1,0:T(8,128)(2,1)}), bf16[128,256]{1,0:T(8,128)(2,1)}) %all-reduce.3.cloned.1.call-update) | async-done | bytes 65552 | tf_op jit(solution)/shard_map/psum | solution.py:130
  352.4 0.0 all-gather.2.cloned.1.call-update
  353.0 0.1 dynamic_slice.21
  353.1 0.1 dynamic_slice.22
  353.2 0.8 dynamic_slice.25
  354.0 0.8 dynamic_slice.26
  354.7 0.1 broadcast_bitcast_fusion
  354.8 0.1 broadcast_bitcast_fusion.1
  354.9 0.6 mul.196
  355.5 0.6 eq.32
  356.1 0.1 broadcast_compare_fusion
  356.2 58.5 %all-gather.2.cloned.1.call-done = bf16[2048,256]{1,0:T(8,128)(2,1)} async-done(((bf16[128,256]{1,0:T(8,128)(2,1)}), bf16[2048,256]{1,0:T(8,128)(2,1)}) %all-gather.2.cloned.1.call-update) | async-done | bytes 1048592 | tf_op jit(solution)/shard_map/all_gather | solution.py:131
  414.8 0.7 dynamic-slice_convert_fusion.3
  415.5 0.9 dynamic-slice_convert_fusion.2
  416.3 2.1 fusion.11
  418.5 3.1 multiply_reduce_fusion.3
  421.6 0.6 add_rsqrt_fusion
  422.3 0.5 copy-done.9
  422.8 0.0 copy-done.10
  422.8 4.7 multiply_convert_fusion.3
  427.6 1.2 fusion.30
  428.8 4.0 fusion.1
  432.8 9.3 %multiply_reduce_fusion.4 = (f32[4096]{0:T(1024)}, f32[4096]{0:T(1024)}, f32[4096,128]{1,0:T(8,128)}) fusion(f32[128]{0:T(128)} %param.21, f32[4096]{0:T(1024)} %bitcast.79, f32[4096]{0:T(1024)} %bitcast.81, f32[128]{0:T(128)} %copy-done.17, f32[128]{0:T(128)} %copy-done.15, pred[4096]{0:T(1024)(128)(4,1)} %eq.32, ...), kind=kOutput, calls=%fused_computation.20 | convolution fusion | flops 1097326592 | bytes 13981184 | tf_op jit(solution)/shard_map/dot_general | solution.py:54
  442.1 0.7 broadcast_multiply_fusion.1
  442.9 9.0 %multiply_reduce_fusion = (f32[256,128]{1,0:T(8,128)S(1)}, f32[16,128]{1,0:T(8,128)}, bf16[16,256,128]{2,1,0:T(8,128)(2,1)}) fusion(f32[16,128]{1,0:T(8,128)} %copy-done.6, f32[16,256]{1,0:T(8,128)S(1)} %div.39, f32[16,256]{1,0:T(8,128)} %copy-done.4, f32[128]{0:T(128)} %copy-done.17, f32[128]{0:T(128)} %copy-done.15, pred[16,256]{1,0:T(8,128)(4,1)} %copy-done.8, ...), kind=kLoop, calls=%fused_computation.12 | loop fusion | flops 13596672 | bytes 8754688 | tf_op jit(solution)/shard_map/reduce_sum | solution.py:65
  451.9 0.1 broadcast_in_dim.87
  452.0 0.6 copy-done.13
  452.6 0.5 dynamic_update_slice.6
  453.1 0.0 copy-start.3
  453.1 120.7 %all-reduce.4 = bf16[2048,256]{1,0:T(8,128)(2,1)} all-reduce(f32[2048,256]{1,0:T(8,128)S(1)} %constant_dynamic-update-slice_fusion), channel_id=1, replica_groups=mesh['lm'=16,'prow'=4,'pcol'=8] {'lm','prow','pcol'}, use_global_device_ids=true, to_apply=%region_10.11 | all-reduce | flops 524288 | bytes 3145728 | tf_op jit(solution)/shard_map/psum | solution.py:163
  573.8 1.6 convolution_convert_fusion.2
  (47 shorter events, 0.2 us)
Async XLA Ops:
  7.2 57.3 %copy-start = (bf16[128,5120]{1,0:T(8,128)(2,1)S(1)}, bf16[128,5120]{1,0:T(8,128)(2,1)}, u32[]{:S(2)}) copy-start(bf16[128,5120]{1,0:T(8,128)(2,1)} %param.18) | copy-start | bytes 3932164
  7.2 34.8 %copy-start.12 = (bf16[128,128]{1,0:T(8,128)(2,1)S(1)}, bf16[128,128]{1,0:T(8,128)(2,1)}, u32[]{:S(2)}) copy-start(bf16[128,128]{1,0:T(8,128)(2,1)} %param.16) | copy-start | bytes 98308
  7.2 217.5 %reduce-scatter.2.cloned.1.call-start = ((), (), s32[]{:S(2)}) async-start(), calls=%async_computation.1 | async-start | bytes 1351680 | tf_op jit(solution)/shard_map/reduce_scatter | solution.py:120
  64.4 160.3 %copy-start.2 = (bf16[160,256]{1,0:T(8,128)(2,1)S(1)}, bf16[160,256]{1,0:T(8,128)(2,1)}, u32[]{:S(2)}) copy-start(bf16[160,256]{1,0:T(8,128)(2,1)} %param.19) | copy-start | bytes 245764
  64.4 160.3 %copy-start.11 = (bf16[128,160]{0,1:T(8,128)(2,1)S(1)}, bf16[128,160]{0,1:T(8,128)(2,1)}, u32[]{:S(2)}) copy-start(bf16[128,160]{0,1:T(8,128)(2,1)} %param.17) | copy-start | bytes 122884
  64.4 291.7 %copy-start.19 = (f32[2,128]{1,0:T(2,128)S(1)}, f32[2,128]{1,0:T(2,128)}, u32[]{:S(2)}) copy-start(f32[2,128]{1,0:T(2,128)} %param.20) | copy-start | bytes 3076
  66.4 285.9 %all-reduce.3.cloned.1.call-start = ((), (), s32[]{:S(2)}) async-start(), calls=%async_computation.2 | async-start | bytes 131072 | tf_op jit(solution)/shard_map/psum | solution.py:130
  226.4 188.4 %all-gather.2.cloned.1.call-start = ((), (), s32[]{:S(2)}) async-start(), calls=%async_computation.3 | async-start | bytes 1114112 | tf_op jit(solution)/shard_map/all_gather | solution.py:131
  356.1 62.3 %copy-start.15 = (f32[128]{0:T(128)}, f32[128]{0:T(128)S(1)}, u32[]{:S(2)}) copy-start(f32[128]{0:T(128)S(1)} %get-tuple-element.13) | copy-start | bytes 1540
  356.1 62.3 %copy-start.17 = (f32[128]{0:T(128)}, f32[128]{0:T(128)S(1)}, u32[]{:S(2)}) copy-start(f32[128]{0:T(128)S(1)} %get-tuple-element.14) | copy-start | bytes 1540
  356.2 62.2 %copy-start.8 = (pred[16,256]{1,0:T(8,128)(4,1)}, pred[16,256]{1,0:T(8,128)(4,1)S(1)}, u32[]{:S(2)}) copy-start(pred[16,256]{1,0:T(8,128)(4,1)S(1)} %broadcast_compare_fusion) | copy-start | bytes 12292
  414.8 8.1 %copy-start.7 = (f32[4096]{0:T(1024)S(1)}, f32[4096]{0:T(1024)}, u32[]{:S(2)}) copy-start(f32[4096]{0:T(1024)} %mul.196) | copy-start | bytes 49156
  414.8 8.1 %copy-start.14 = (pred[4096]{0:T(1024)(128)(4,1)S(1)}, pred[4096]{0:T(1024)(128)(4,1)}, u32[]{:S(2)}) copy-start(pred[4096]{0:T(1024)(128)(4,1)} %eq.32) | copy-start | bytes 12292
  415.5 6.8 %copy-start.6 = (f32[16,128]{1,0:T(8,128)}, f32[16,128]{1,0:T(8,128)S(1)}, u32[]{:S(2)}) copy-start(f32[16,128]{1,0:T(8,128)S(1)} %dynamic-slice_convert_fusion.3) | copy-start | bytes 24580
  418.5 3.8 copy-start.4
  418.5 4.4 copy-start.16
  418.5 4.4 copy-start.18
  421.6 6.0 %copy-start.5 = (bf16[128,512]{1,0:T(8,128)(2,1)S(1)}, bf16[128,512]{1,0:T(8,128)(2,1)}, u32[]{:S(2)}) copy-start(bf16[128,512]{1,0:T(8,128)(2,1)} %param.22) | copy-start | bytes 393220
  422.2 0.6 copy-start.9
  422.2 0.6 copy-start.10
  427.6 1.3 copy-start.20
  428.8 4.0 copy-start.1
  451.9 0.7 copy-start.13
  453.1 120.7 %copy-start.3 = (bf16[160,256]{1,0:T(8,128)(2,1)S(1)}, bf16[160,256]{1,0:T(8,128)(2,1)}, u32[]{:S(2)}) copy-start(bf16[160,256]{1,0:T(8,128)(2,1)} %param.19) | copy-start | bytes 245764
Sparse Core Ops, SparseCore 0:
  66.6 158.1 reduce-scatter.1
  228.9 123.3 all-reduce.2
  354.4 60.2 all-gather.1
where the time goes:
time: 583 us; the launch traced here: 582 us
  waiting for transfers between devices  343 us (59%)
  blocking collectives  175 us (30%)
  other arithmetic  24.9 us (4%)
  matrix products  20.9 us (4%)
  between operations  14.7 us (3%)
    reduce_scatter x1, waiting for transfers between devices, body(): lax.psum_scatter(lax.dot_general(out_proj, attended, (((0,), (1,)), ((),...  158 us
    psum x1, waiting for transfers between devices, body(): projected_here = lax.psum(proj_terms.astype(jnp.bfloat16), ('prow', 'pcol'))  126 us
    psum x1, blocking collectives, body(): summed_all = lax.psum(local, ('lm', 'prow', 'pcol'))  121 us
    all_gather x1, waiting for transfers between devices, body(): projected = lax.all_gather(projected_here, 'lm', axis=0, tiled=True)  58.5 us
    all_gather x1, blocking collectives, body(): key_piece = lax.all_gather(keys, 'lm', axis=0, tiled=True)  32 us
    all_gather x1, blocking collectives, body(): value_piece = lax.all_gather(values, 'lm', axis=0, tiled=True)  22.2 us
  transfers between devices with their start and end apart: 3, of which 3 were waited for; matrix products, arithmetic and copies ran while one was open for 1% of the time, Pallas kernels for 0%

commit v1 on v0

v1 whole, which is shorter than its diff:
```python
import functools
import math

import jax
import jax.numpy as jnp
from jax import lax
from jax.experimental import pallas as pl
from jax.experimental.pallas import tpu as pltpu
from jax.sharding import PartitionSpec as P

BF = jnp.bfloat16
F32 = jnp.float32
MESH = pl.DeviceIdType.MESH
E = 128
W = 256


def nn(a, b):
    return lax.dot_general(a, b, (((1,), (0,)), ((), ())), preferred_element_type=F32)


def nt(a, b):
    return lax.dot_general(a, b, (((1,), (1,)), ((), ())), preferred_element_type=F32)


def grid_of(rows, columns):
    row = lax.broadcasted_iota(jnp.int32, (rows, columns), 0)
    column = lax.broadcasted_iota(jnp.int32, (rows, columns), 1)
    return row, column


def one_hot(hit):
    return jnp.where(hit, 1.0, 0.0).astype(BF)


def bits(n):
    return n.bit_length() - 1


class Place:
    def __init__(self, sizes):
        self.nz, self.pr, self.pc = sizes
        self.np = self.pr * self.pc
        self.z = lax.axis_index("lm")
        self.prow = lax.axis_index("prow")
        self.pcol = lax.axis_index("pcol")
        self.q = self.prow * self.pc + self.pcol

    def plane_peer(self, i):
        peer = lax.rem(self.q + i, self.np)
        return peer, (self.z, peer // self.pc, lax.rem(peer, self.pc))

    def z_peer(self, i):
        peer = lax.rem(self.z + i, self.nz)
        return peer, (peer, self.prow, self.pcol)

    def signal_all(self, barrier):
        def plane(i, carry):
            pl.semaphore_signal(
                barrier, inc=1, device_id=self.plane_peer(i)[1], device_id_type=MESH
            )
            return carry

        def column(i, carry):
            pl.semaphore_signal(barrier, inc=1, device_id=self.z_peer(i)[1], device_id_type=MESH)
            return carry

        lax.fori_loop(1, self.np, plane, 0)
        lax.fori_loop(1, self.nz, column, 0)

    def wait_all(self, barrier):
        pl.semaphore_wait(barrier, self.np + self.nz - 2)

    def to_plane(self, source, target, send_sem, recv_sem):
        def step(i, carry):
            peer, device = self.plane_peer(i)
            pltpu.make_async_remote_copy(
                src_ref=source(peer),
                dst_ref=target.at[self.q],
                send_sem=send_sem,
                recv_sem=recv_sem,
                device_id=device,
                device_id_type=MESH,
            ).start()
            return carry

        lax.fori_loop(1, self.np, step, 0)

    def to_column(self, source, target, send_sem, recv_sem):
        def step(i, carry):
            peer, device = self.z_peer(i)
            pltpu.make_async_remote_copy(
                src_ref=source(peer),
                dst_ref=target.at[self.z],
                send_sem=send_sem,
                recv_sem=recv_sem,
                device_id=device,
                device_id_type=MESH,
            ).start()
            return carry

        lax.fori_loop(1, self.nz, step, 0)


def wait_bytes(buffer, count, sem):
    part = buffer.at[pl.ds(0, count)]
    pltpu.make_async_copy(part, part, sem).wait()


def forward_kernel(
    sizes,
    start_ref,
    mask_ref,
    q_ref,
    k_ref,
    v_ref,
    res_ref,
    op_hbm,
    pp_ref,
    ab_ref,
    op,
    kbuf,
    vbuf,
    sbuf,
    perm,
    pick,
    place_rows,
    presidual,
    ppmsg,
    ppg,
    w2acc,
    w2msg,
    w2g,
    pmsg,
    pbuf,
    tmsg,
    zbuf,
    msg,
    rbuf,
    op_sem,
    ring_send,
    ring_recv,
    send_sem,
    recv_sem,
):
    me = Place(sizes)
    nz, pr, pc, np_ = me.nz, me.pr, me.pc, me.np
    z, q = me.z, me.q
    rb = q_ref.shape[0]
    fd = pp_ref.shape[0]
    wz = W // nz
    columns = 8 * np_
    slab_plane = 2 * np_
    slab_tile = slab_plane // pr
    log_np = bits(np_)

    barrier = pltpu.get_barrier_semaphore()
    me.signal_all(barrier)
    fetch = pltpu.make_async_copy(op_hbm, op, op_sem)
    fetch.start()
    kbuf[z] = k_ref[...]
    vbuf[z] = v_ref[...]

    row, column = grid_of(wz, W)
    mine = one_hot(column == row + z * wz)
    piece = nt(mine, pp_ref[...]).astype(BF)
    row, column = grid_of(fd, W)
    shift = one_hot(column == row + ((fd * q) & 127))
    piece = nn(piece, shift).astype(BF)
    ppmsg[...] = piece
    ppg[q] = piece

    me.wait_all(barrier)

    def ring(chain, s):
        buf = kbuf if chain < 2 else vbuf
        way = 1 if chain % 2 == 0 else -1
        block = lax.rem(z - way * s + nz, nz)
        peer = lax.rem(z + way + nz, nz)
        return pltpu.make_async_remote_copy(
            src_ref=buf.at[block],
            dst_ref=buf.at[block],
            send_sem=ring_send.at[chain, s],
            recv_sem=ring_recv.at[chain, s],
            device_id=(peer, me.prow, me.pcol),
            device_id_type=MESH,
        )

    steps = (nz // 2, nz - 1 - nz // 2)
    for chain in range(4):
        if steps[chain % 2] > 0:
            ring(chain, 0).start()
    me.to_plane(lambda peer: ppmsg, ppg, send_sem.at[0], recv_sem.at[0])

    scale = 1.0 / math.sqrt(E)

    def score(block):
        raw = nt(q_ref[...], kbuf[block]) * scale
        live = mask_ref[pl.ds(block, 1), :]
        sbuf[block] = jnp.where(live > 0, raw, -1e30)

    row, column = grid_of(8 * np_, rb)
    perm[...] = one_hot(column == (row & 3) * np_ + (row >> 3))
    w0 = start_ref[0] + z * slab_plane
    r0 = w0 + ((q - w0) & (np_ - 1))
    k0 = r0 >> log_np
    row, column = grid_of(pc * 16, 8 * nz)
    sub = row & 15
    right_hit = (sub < 8) & (column == (2 * (row >> 4) + (sub >> 2)) * 8 + 4 + (sub & 3))
    kk = k0 + (sub - 8)
    left_hit = ((sub == 8) | (sub == 9)) & (column == (kk >> 2) * 8 + (kk & 3))
    pick[...] = one_hot(right_hit | left_hit)
    row, column = grid_of(columns + slab_tile, 16 * np_)
    first = w0 + me.prow * slab_tile
    second_half = jnp.where(me.prow >= pr // 2, 1, 0)
    right_hit = (row < columns) & (column == (row & (np_ - 1)) * 16 + (row >> log_np))
    left_hit = (row >= columns) & (
        column == ((first + row - columns) & (np_ - 1)) * 16 + 8 + second_half
    )
    place_rows[...] = one_hot(right_hit | left_hit)
    rows_twice = nn(perm[...], res_ref[...]).astype(BF)
    both = nn(rows_twice, pp_ref[...])
    row, column = grid_of(8 * np_, E)
    is_left = (row & 7) < 4
    presidual[...] = jnp.where(is_left, both[:, :E], both[:, E:])

    score(z)
    w2acc[...] = jnp.zeros_like(w2acc)
    groups = min(4, np_)
    per_group = np_ // groups

    def w2_group(g):
        total = w2acc[...]
        for i in range(per_group):
            chunk = g * per_group + i
            at = pl.multiple_of(((fd * chunk) >> 7) << 7, 128)
            total = total + nt(op[:, pl.ds(at, W)], ppg[chunk])
        w2acc[...] = total

    def ring_step(s):
        for chain in (0, 1):
            if s < steps[chain]:
                ring(chain, s).wait_recv()
                if s + 1 < steps[chain]:
                    ring(chain, s + 1).start()
        for chain in (2, 3):
            if s < steps[chain % 2]:
                ring(chain, s).wait_recv()
                if s + 1 < steps[chain % 2]:
                    ring(chain, s + 1).start()
        if s < steps[0]:
            score(lax.rem(z - 1 - s + nz, nz))
        if s < steps[1]:
            score(lax.rem(z + 1 + s, nz))

    def w2_send():
        w2 = w2acc[...].astype(BF)
        row, column = grid_of(wz, wz)
        turned = nt(one_hot(row == column), w2).astype(BF)
        w2msg[...] = turned
        w2g[z] = turned
        me.to_column(lambda peer: w2msg, w2g, send_sem.at[1], recv_sem.at[1])

    done = 0
    for s in range(steps[0]):
        ring_step(s)
        if s == 0:
            fetch.wait()
            wait_bytes(ppg, np_ - 1, recv_sem.at[0])
        while done < groups and (done < s + 1 or s + 1 == steps[0]):
            w2_group(done)
            done += 1
            if done == groups:
                w2_send()

    def widest(b, carry):
        return jnp.maximum(carry, sbuf[b])

    top = lax.fori_loop(0, nz, widest, jnp.full((rb, rb), -1e30, F32))
    top = jnp.max(top, axis=1, keepdims=True)

    def soften(b, carry):
        below, above = carry
        shifted = jnp.exp(sbuf[b] - top)
        return below + shifted, above + nn(shifted.astype(BF), vbuf[b])

    below, above = lax.fori_loop(
        0, nz, soften, (jnp.zeros((rb, rb), F32), jnp.zeros((rb, E), F32))
    )
    attended = (above / jnp.sum(below, axis=1, keepdims=True)).astype(BF)

    wait_bytes(w2g, nz - 1, recv_sem.at[1])
    twice = nn(perm[...], attended).astype(BF)
    w2 = w2g[...].reshape(W, E)
    both = nt(twice, w2)
    row, column = grid_of(8 * np_, E)
    is_left = (row & 7) < 4
    terms = jnp.where(is_left, both[:, :E], both[:, E:]) + presidual[...]
    pmsg[...] = terms.reshape(np_, 8, E)
    me.to_plane(lambda peer: pmsg.at[peer], pbuf, send_sem.at[2], recv_sem.at[2])
    pbuf[q] = pmsg[q]
    wait_bytes(pbuf, np_ - 1, recv_sem.at[2])
    projected = jnp.sum(pbuf[...], axis=0).astype(BF).astype(F32)
    tmsg[...] = projected
    zbuf[z] = projected
    me.to_column(lambda peer: tmsg, zbuf, send_sem.at[3], recv_sem.at[3])
    wait_bytes(zbuf, nz - 1, recv_sem.at[3])
    chosen = nn(pick[...], zbuf[...].reshape(8 * nz, E).astype(BF)).astype(BF)
    msg[...] = chosen.reshape(pc, 16, E)
    me.to_plane(
        lambda peer: msg.at[lax.rem(peer, pc)], rbuf, send_sem.at[4], recv_sem.at[4]
    )
    rbuf[q] = msg[me.pcol]
    wait_bytes(rbuf, np_ - 1, recv_sem.at[4])
    ab_ref[...] = nn(place_rows[...], rbuf[...].reshape(16 * np_, E))

    for chain in range(4):
        for s in range(steps[chain % 2]):
            ring(chain, s).wait_send()
    wait_bytes(ppg, np_ - 1, send_sem.at[0])
    wait_bytes(w2g, nz - 1, send_sem.at[1])
    wait_bytes(pbuf, np_ - 1, send_sem.at[2])
    wait_bytes(zbuf, nz - 1, send_sem.at[3])
    wait_bytes(rbuf, np_ - 1, send_sem.at[4])


def forward(sizes, start, mask, queries, keys, values, residual, out_proj, pair_proj):
    nz, pr, pc = sizes
    np_ = pr * pc
    rb = queries.shape[0]
    d = out_proj.shape[1]
    columns = 8 * np_
    tile = 2 * np_ // pr
    wz = W // nz
    vmem = pl.BlockSpec(memory_space=pltpu.VMEM)
    return pl.pallas_call(
        functools.partial(forward_kernel, sizes),
        out_shape=jax.ShapeDtypeStruct((columns + tile, E), F32),
        in_specs=[pl.BlockSpec(memory_space=pltpu.SMEM)]
        + [vmem] * 5
        + [pl.BlockSpec(memory_space=pl.ANY), vmem],
        out_specs=vmem,
        scratch_shapes=[
            pltpu.VMEM((E, d), BF),
            pltpu.VMEM((nz, rb, E), BF),
            pltpu.VMEM((nz, rb, E), BF),
            pltpu.VMEM((nz, rb, rb), F32),
            pltpu.VMEM((8 * np_, rb), BF),
            pltpu.VMEM((pc * 16, 8 * nz), BF),
            pltpu.VMEM((columns + tile, 16 * np_), BF),
            pltpu.VMEM((8 * np_, E), F32),
            pltpu.VMEM((wz, W), BF),
            pltpu.VMEM((np_, wz, W), BF),
            pltpu.VMEM((E, wz), F32),
            pltpu.VMEM((wz, E), BF),
            pltpu.VMEM((nz, wz, E), BF),
            pltpu.VMEM((np_, 8, E), F32),
            pltpu.VMEM((np_, 8, E), F32),
            pltpu.VMEM((8, E), F32),
            pltpu.VMEM((nz, 8, E), F32),
            pltpu.VMEM((pc, 16, E), BF),
            pltpu.VMEM((np_, 16, E), BF),
            pltpu.SemaphoreType.DMA,
            pltpu.SemaphoreType.DMA((4, max(1, nz // 2))),
            pltpu.SemaphoreType.DMA((4, max(1, nz // 2))),
            pltpu.SemaphoreType.DMA((5,)),
            pltpu.SemaphoreType.DMA((5,)),
        ],
        compiler_params=pltpu.CompilerParams(
            collective_id=0, has_side_effects=True, vmem_limit_bytes=32 << 20
        ),
        name="attend_and_project",
    )(start, mask, queries, keys, values, residual, out_proj, pair_proj)


def pair_kernel(
    rows_here,
    start_ref,
    mask_ref,
    chain_ref,
    ab_ref,
    live_ref,
    same_ref,
    bias_ref,
    gain_ref,
    w_in_ref,
    w_out_ref,
    cot_ref,
    out_ref,
    grad_ref,
    w_half,
    w_out_half,
):
    columns = cot_ref.shape[1]
    per_step = cot_ref.shape[0]
    step = pl.program_id(0)

    @pl.when(step == 0)
    def _():
        grad_ref[...] = jnp.zeros_like(grad_ref)
        w_half[...] = (w_in_ref[...].astype(F32) * 0.5).astype(BF)
        w_out_half[...] = (w_out_ref[...].astype(F32) * 0.5).astype(BF)

    first = start_ref[0] + (lax.axis_index("lm") * lax.axis_size("prow") + lax.axis_index("prow")) * rows_here
    right = ab_ref[pl.ds(0, columns), :]
    live_columns = live_ref[...]
    gain = gain_ref[...]
    for i in range(per_step):
        t = step * per_step + i
        left = ab_ref[pl.ds(columns + t, 1), :]
        live = live_columns * mask_ref[first + t].astype(F32)
        bias = jnp.where(same_ref[...] == chain_ref[first + t], bias_ref[1:2, :], bias_ref[0:1, :])
        seed = live * (left * right + bias)
        centre = seed - jnp.mean(seed, axis=1, keepdims=True)
        inverse = lax.rsqrt(jnp.mean(centre * centre, axis=1, keepdims=True) + 1e-05)
        normed = centre * inverse
        scaled = (normed * gain).astype(BF)
        half = nn(scaled, w_half[...])
        turned = jnp.tanh(half)
        raised = 1.0 + turned
        act = half * raised
        cot = cot_ref[i]
        d_act = nt(cot, w_out_half[...])
        d_hidden = (d_act * (raised + act * (1.0 - turned))).astype(BF)
        out_ref[i] = (seed + nn(act.astype(BF), w_out_ref[...])).astype(BF)
        d_normed = nt(d_hidden, w_in_ref[...]) * gain
        d_seed = cot.astype(F32) + inverse * (
            d_normed
            - jnp.mean(d_normed, axis=1, keepdims=True)
            - normed * jnp.mean(d_normed * normed, axis=1, keepdims=True)
        )
        d_prod = d_seed * live
        grad_ref[pl.ds(0, columns), :] += d_prod * left
        grad_ref[pl.ds(columns + t, 1), :] = jnp.sum(d_prod * right, axis=0, keepdims=True)


def pair(start, mask, chain, ab, live_columns, chain_columns, chain_bias, gain, w_in, w_out, cot):
    rows, columns, width = cot.shape
    per_step = 2
    hidden = w_in.shape[1]
    smem = pl.BlockSpec(memory_space=pltpu.SMEM)

    def whole(a):
        return pl.BlockSpec(a.shape, lambda i: (0,) * a.ndim)

    block = pl.BlockSpec((per_step, columns, width), lambda i: (i, 0, 0))
    return pl.pallas_call(
        functools.partial(pair_kernel, rows),
        grid=(rows // per_step,),
        out_shape=(
            jax.ShapeDtypeStruct(cot.shape, BF),
            jax.ShapeDtypeStruct((columns + rows, width), F32),
        ),
        in_specs=[smem, smem, smem]
        + [whole(a) for a in (ab, live_columns, chain_columns, chain_bias, gain, w_in, w_out)]
        + [block],
        out_specs=(block, pl.BlockSpec((columns + rows, width), lambda i: (0, 0))),
        scratch_shapes=[pltpu.VMEM((width, hidden), BF), pltpu.VMEM((hidden, width), BF)],
        compiler_params=pltpu.CompilerParams(vmem_limit_bytes=32 << 20),
        name="pair_transition",
    )(start, mask, chain, ab, live_columns, chain_columns, chain_bias, gain, w_in, w_out, cot)


def backward_kernel(
    sizes,
    start_ref,
    grad_ref,
    pp_ref,
    lm_ref,
    msg,
    gbuf,
    zmsg,
    hbuf,
    fmsg,
    fbuf,
    send_sem,
    recv_sem,
):
    me = Place(sizes)
    nz, pr, pc, np_ = me.nz, me.pr, me.pc, me.np
    z, q = me.z, me.q
    rb = lm_ref.shape[0]
    columns = 8 * np_
    slab_plane = 2 * np_
    slab_tile = slab_plane // pr
    log_np = bits(np_)
    barrier = pltpu.get_barrier_semaphore()
    me.signal_all(barrier)

    w0 = start_ref[0] + z * slab_plane
    r0 = w0 + ((q - w0) & (np_ - 1))
    k0 = r0 >> log_np
    first = w0 + me.prow * slab_tile
    second_half = jnp.where(me.prow >= pr // 2, 1, 0)
    row, column = grid_of(16 * np_, columns + slab_tile)
    sub = row & 15
    owner = row >> 4
    right_hit = (sub < 8) & (column == sub * np_ + owner)
    left_hit = (
        (sub == 8 + second_half)
        & (column >= columns)
        & (((first + column - columns) & (np_ - 1)) == owner)
    )
    spread = one_hot(right_hit | left_hit)
    msg[...] = nn(spread, grad_ref[...].astype(BF)).astype(BF).reshape(np_, 16, E)
    me.wait_all(barrier)
    me.to_plane(lambda peer: msg.at[peer], gbuf, send_sem.at[0], recv_sem.at[0])
    gbuf[q] = msg[q]
    wait_bytes(gbuf, np_ - 1, recv_sem.at[0])
    by_column = jnp.sum(gbuf[...].astype(F32).reshape(pr, pc, 16, E), axis=0)
    over_columns = jnp.sum(by_column, axis=0)
    left0 = over_columns[8:9, :]
    left1 = over_columns[9:10, :]
    sub, _ = grid_of(8, E)
    for other in range(nz):
        k = 4 * other + (sub & 3)
        lefts = jnp.where(k == k0, left0, jnp.where(k == k0 + 1, left1, 0.0))
        zmsg[other] = jnp.where((sub >> 2) == other % 2, by_column[other // 2, 0:8, :], lefts)
    me.to_column(lambda peer: zmsg.at[peer], hbuf, send_sem.at[1], recv_sem.at[1])
    hbuf[z] = zmsg[z]
    wait_bytes(hbuf, nz - 1, recv_sem.at[1])
    tile = jnp.sum(hbuf[...], axis=0).astype(BF).astype(F32)
    fmsg[...] = tile
    fbuf[q] = tile
    me.to_plane(lambda peer: fmsg, fbuf, send_sem.at[2], recv_sem.at[2])
    odd = z & 1
    row, column = grid_of(rb, 8 * np_)
    base = (row & (np_ - 1)) * 8 + (row >> log_np)
    left_pick = one_hot(column == base + 4 * (1 - odd))
    right_pick = one_hot(column == base + 4 * odd)
    wait_bytes(fbuf, np_ - 1, recv_sem.at[2])
    tiles = fbuf[...].reshape(8 * np_, E).astype(BF)
    left = nn(left_pick, tiles).astype(BF)
    right = nn(right_pick, tiles).astype(BF)
    lm_ref[...] = (nt(left, pp_ref[:, :E]) + nt(right, pp_ref[:, E:])).astype(BF)
    wait_bytes(gbuf, np_ - 1, send_sem.at[0])
    wait_bytes(hbuf, nz - 1, send_sem.at[1])
    wait_bytes(fbuf, np_ - 1, send_sem.at[2])


def backward(sizes, rb, start, grads, pair_proj):
    nz, pr, pc = sizes
    np_ = pr * pc
    vmem = pl.BlockSpec(memory_space=pltpu.VMEM)
    return pl.pallas_call(
        functools.partial(backward_kernel, sizes),
        out_shape=jax.ShapeDtypeStruct((rb, pair_proj.shape[0]), BF),
        in_specs=[pl.BlockSpec(memory_space=pltpu.SMEM), vmem, vmem],
        out_specs=vmem,
        scratch_shapes=[
            pltpu.VMEM((np_, 16, E), BF),
            pltpu.VMEM((np_, 16, E), BF),
            pltpu.VMEM((nz, 8, E), F32),
            pltpu.VMEM((nz, 8, E), F32),
            pltpu.VMEM((8, E), F32),
            pltpu.VMEM((np_, 8, E), F32),
            pltpu.SemaphoreType.DMA((3,)),
            pltpu.SemaphoreType.DMA((3,)),
        ],
        compiler_params=pltpu.CompilerParams(
            collective_id=1, has_side_effects=True, vmem_limit_bytes=32 << 20
        ),
        name="reduce_gradients",
    )(start, grads, pair_proj)


def body(
    sizes,
    queries,
    keys,
    values,
    residual,
    out_proj,
    pair_proj,
    chain_bias,
    ln_gain,
    w_in,
    w_out,
    pair_cot,
    residue_mask,
    chain_ids,
    slab_start,
):
    rb = queries.shape[0]
    columns = pair_cot.shape[1]
    first_column = lax.axis_index("pcol") * columns
    live = residue_mask.astype(F32)
    live_columns = jnp.broadcast_to(
        lax.dynamic_slice_in_dim(live, first_column, columns)[:, None], (columns, E)
    )
    chain_columns = jnp.broadcast_to(
        lax.dynamic_slice_in_dim(chain_ids, first_column, columns)[:, None], (columns, E)
    )
    ab = forward(
        sizes,
        slab_start,
        residue_mask.reshape(sizes[0], rb),
        queries,
        keys,
        values,
        residual,
        out_proj,
        pair_proj,
    )
    pair_out, grads = pair(
        slab_start,
        residue_mask,
        chain_ids,
        ab,
        live_columns,
        chain_columns,
        chain_bias,
        ln_gain.reshape(1, E),
        w_in,
        w_out,
        pair_cot,
    )
    lm_grad = backward(sizes, rb, slab_start, grads, pair_proj)
    return pair_out, lm_grad


def solution(mesh):
    sizes = tuple(mesh.shape[name] for name in ("lm", "prow", "pcol"))
    return jax.shard_map(
        functools.partial(body, sizes),
        mesh=mesh,
        in_specs=(
            P("lm", ("prow", "pcol")),
            P("lm", ("prow", "pcol")),
            P("lm", ("prow", "pcol")),
            P("lm", ("prow", "pcol")),
            P(("prow", "pcol"), None),
            P(("prow", "pcol"), None),
            P(),
            P(),
            P(),
            P(),
            P(("lm", "prow"), "pcol", None),
            P(),
            P(),
            P(),
        ),
        out_specs=(P(("lm", "prow"), "pcol", None), P("lm", ("prow", "pcol"))),
        check_vma=False,
    )
```

time: 583 us -> 115 us (0.20)
  waiting for transfers between devices: 343 us -> 0 us
  blocking collectives: 175 us -> 0 us
  Pallas kernels: 0 us -> 105 us
  other arithmetic: 24.9 us -> 0.76 us
  matrix products: 20.9 us -> 0 us
  between operations: 14.7 us -> 1.44 us
    reduce_scatter x1 -> x0, waiting for transfers between devices: 158 us -> none  [body(): lax.psum_scatter(lax.dot_general(out_proj, attended, (((0,), (1,)), ((),...]
    psum x1 -> x0, waiting for transfers between devices: 126 us -> none  [body(): projected_here = lax.psum(proj_terms.astype(jnp.bfloat16), ('prow', 'pcol'))]
    psum x1 -> x0, blocking collectives: 121 us -> none  [body(): summed_all = lax.psum(local, ('lm', 'prow', 'pcol'))]
    pallas_call x0 -> x3, Pallas kernels: none -> 105 us  [the longest x1 68.8 us: forward(): pl.pallas_call(functools.partial(forward_kernel, sizes), out_shape=jax.Sh...]
    all_gather x1 -> x0, waiting for transfers between devices: 58.5 us -> none  [body(): projected = lax.all_gather(projected_here, 'lm', axis=0, tiled=True)]
    all_gather x2 -> x0, blocking collectives: 54.2 us -> none  [the longest x1 32 us: body(): key_piece = lax.all_gather(keys, 'lm', axis=0, tiled=True)]
    dot_general x7 -> x0, matrix products: 20.9 us -> none  [the longest x1 9.35 us: pair_terms(): lax.dot_general(d_hidden, w_in, (((1,), (1,)), ((), ())), preferred_eleme...]
    reduce_sum x4 -> x0, other arithmetic: 14.4 us -> none  [the longest x1 8.96 us: pair_terms(): grad_columns = jnp.sum(d_prod * a_float[:, None, :], axis=0)]
  transfers between devices with their start and end apart: 3 -> 0, of which waited for: 3 -> 0; matrix products, arithmetic and copies ran while one was open for 1% -> 0% of each run, Pallas kernels for 0% -> 0%
where the time goes in v1:
time: 115 us
  Pallas kernels  105 us (91%)
  local copies, waits for them, and re-layouts  7.73 us (7%)
  between operations  1.44 us (1%)
    pallas_call x1, Pallas kernels, forward(): pl.pallas_call(functools.partial(forward_kernel, sizes), out_shape=jax.Sh...  68.8 us
    pallas_call x1, Pallas kernels, backward(): pl.pallas_call(functools.partial(backward_kernel, sizes), out_shape=jax.S...  25.1 us
    pallas_call x1, Pallas kernels, pair(): pl.pallas_call(functools.partial(pair_kernel, rows), grid=(rows // per_st...  10.9 us
    unnamed x26, local copies, waits for them, and re-layouts  6.79 us

profile of v1, /device:TPU:1, one launch (start us, length us, event | category | flops | bytes accessed | tf_op | source)
XLA Modules:
  0.0 114.6 jit_solution(4361984838064895543)
XLA Ops:
  0.6 0.0 copy-start.3
  1.3 0.8 dynamic_slice.7
  2.1 0.8 dynamic-slice_convert_fusion
  2.8 0.9 copy.16.res_ref
  3.7 0.0 copy-start
  3.7 1.3 %copy-done = bf16[128,5120]{1,0:T(8,128)(2,1)S(1)} copy-done((bf16[128,5120]{1,0:T(8,128)(2,1)S(1)}, bf16[128,5120]{1,0:T(8,128)(2,1)}, u32[]{:S(2)}) %copy-start) | copy-done | bytes 1310744
  5.1 0.0 copy-start.2
  5.1 0.9 copy-done.2
  5.9 0.0 copy-start.5
  5.9 0.7 copy-done.5
  6.6 0.0 copy-start.6
  6.6 0.8 copy-done.6
  7.4 0.0 copy-start.7
  7.4 0.8 copy-done.7
  8.2 0.0 copy-start.8
  8.2 0.8 copy-done.8
  8.9 0.0 copy-start.1
  8.9 0.0 copy-start.4
  8.9 0.0 copy-start.9
  8.9 0.0 copy-start.10
  8.9 0.0 copy-start.11
  8.9 68.8 %attend_and_project.1.ab_ref = f32[272,128]{1,0:T(8,128)S(1)} custom-call(s32[1]{0:T(128)S(6)} %copy.18.start_ref, s32[16,128]{1,0:T(8,128)S(1)} %bitcast.2, bf16[128,128]{1,0:T(8,128)(2,1)S(1)} %copy-done.6, bf16[128,128]{1,0:T(8,128)(2,1)S(1)} %copy-done.7, bf16[128,128]{1,0:T(8,128)(2,1)S(1)} %copy-done.8, bf16[128,160]{1,0:T(8,128)(2,1)S(1)} %copy.16.res_ref, ...), custom_call_target="tpu_custom_call" | custom-call | tf_op jit(solution)/shard_map/attend_and_project/pallas_call | solution.py:336
  77.7 0.1 broadcast_in_dim.4.live_ref
  77.8 0.1 broadcast_in_dim.5.same_ref
  77.9 0.0 copy-done.3
  78.0 0.0 copy-done.1
  78.0 0.0 copy-done.4
  78.0 0.0 copy-done.9
  78.0 0.0 copy-done.10
  78.0 0.0 copy-done.11
  78.0 10.9 %pair_transition.1 = (bf16[16,256,128]{2,1,0:T(8,128)(2,1)}, f32[272,128]{1,0:T(8,128)S(1)}) custom-call(s32[1]{0:T(128)S(6)} %copy.18.start_ref, s32[2048]{0:T(1024)S(1)} %copy-done.5, s32[2048]{0:T(1024)S(1)} %copy-done.9, f32[272,128]{1,0:T(8,128)S(1)} %attend_and_project.1.ab_ref, f32[256,128]{1,0:T(8,128)S(1)} %broadcast_in_dim.4.live_ref, ...), custom_call_target="tpu_custom_call" | custom-call | tf_op jit(solution)/shard_map/pair_transition/pallas_call | solution.py:447
  88.9 25.1 %reduce_gradients.1 = bf16[128,160]{1,0:T(8,128)(2,1)S(1)} custom-call(s32[1]{0:T(128)S(6)} %copy.18.start_ref, f32[272,128]{1,0:T(8,128)S(1)} %get-tuple-element.5.grad_ref, bf16[160,256]{1,0:T(8,128)(2,1)S(1)} %copy-done.2), custom_call_target="tpu_custom_call" | custom-call | tf_op jit(solution)/shard_map/reduce_gradients/pallas_call | solution.py:545
  113.9 0.7 copy.17
Async XLA Ops:
  0.6 77.3 %copy-start.3 = (bf16[128,512]{1,0:T(8,128)(2,1)S(1)}, bf16[128,512]{1,0:T(8,128)(2,1)}, u32[]{:S(2)}) copy-start(bf16[128,512]{1,0:T(8,128)(2,1)} %w_in_ref.1) | copy-start | bytes 393220
  3.7 1.3 %copy-start = (bf16[128,5120]{1,0:T(8,128)(2,1)S(1)}, bf16[128,5120]{1,0:T(8,128)(2,1)}, u32[]{:S(2)}) copy-start(bf16[128,5120]{1,0:T(8,128)(2,1)} %op_hbm.1) | copy-start | bytes 3932164
  5.1 0.9 copy-start.2
  5.9 0.7 copy-start.5
  6.6 0.8 copy-start.6
  7.4 0.8 copy-start.7
  8.2 0.8 copy-start.8
  8.9 69.0 %copy-start.1 = (bf16[16,256,128]{2,1,0:T(8,128)(2,1)S(1)}, bf16[16,256,128]{2,1,0:T(8,128)(2,1)}, u32[]{:S(2)}) copy-start(bf16[16,256,128]{2,1,0:T(8,128)(2,1)} %cot_ref.1) | copy-start | bytes 3145732
  8.9 69.1 %copy-start.4 = (bf16[512,128]{1,0:T(8,128)(2,1)S(1)}, bf16[512,128]{1,0:T(8,128)(2,1)}, u32[]{:S(2)}) copy-start(bf16[512,128]{1,0:T(8,128)(2,1)} %w_out_ref.1) | copy-start | bytes 393220
  8.9 69.1 %copy-start.9 = (s32[2048]{0:T(1024)S(1)}, s32[2048]{0:T(1024)}, u32[]{:S(2)}) copy-start(s32[2048]{0:T(1024)} %chain_ref.1) | copy-start | bytes 24580
  8.9 69.1 %copy-start.10 = (f32[2,128]{1,0:T(2,128)S(1)}, f32[2,128]{1,0:T(2,128)}, u32[]{:S(2)}) copy-start(f32[2,128]{1,0:T(2,128)} %bias_ref.1) | copy-start | bytes 3076
  8.9 69.1 %copy-start.11 = (f32[128]{0:T(128)S(1)}, f32[128]{0:T(128)}, u32[]{:S(2)}) copy-start(f32[128]{0:T(128)} %param.21) | copy-start | bytes 1540

commit v2 on v0

v2 whole, which is shorter than its diff:
```python
import functools
import math

import jax
import jax.numpy as jnp
from jax import lax
from jax.experimental import pallas as pl
from jax.experimental.pallas import tpu as pltpu
from jax.sharding import PartitionSpec as P

BF = jnp.bfloat16
F32 = jnp.float32
MESH = pl.DeviceIdType.MESH
E = 128
W = 256


def nn(a, b):
    return lax.dot_general(a, b, (((1,), (0,)), ((), ())), preferred_element_type=F32)


def nt(a, b):
    return lax.dot_general(a, b, (((1,), (1,)), ((), ())), preferred_element_type=F32)


def grid_of(rows, columns):
    row = lax.broadcasted_iota(jnp.int32, (rows, columns), 0)
    column = lax.broadcasted_iota(jnp.int32, (rows, columns), 1)
    return row, column


def one_hot(hit):
    return jnp.where(hit, 1.0, 0.0).astype(BF)


def bits(n):
    return n.bit_length() - 1


class Place:
    def __init__(self, sizes):
        self.nz, self.pr, self.pc = sizes
        self.np = self.pr * self.pc
        self.z = lax.axis_index("lm")
        self.prow = lax.axis_index("prow")
        self.pcol = lax.axis_index("pcol")
        self.q = self.prow * self.pc + self.pcol

    def plane_peer(self, i):
        peer = lax.rem(self.q + i, self.np)
        return peer, (self.z, peer // self.pc, lax.rem(peer, self.pc))

    def z_peer(self, i):
        peer = lax.rem(self.z + i, self.nz)
        return peer, (peer, self.prow, self.pcol)

    def signal_all(self, barrier):
        def plane(i, carry):
            pl.semaphore_signal(
                barrier, inc=1, device_id=self.plane_peer(i)[1], device_id_type=MESH
            )
            return carry

        def column(i, carry):
            pl.semaphore_signal(barrier, inc=1, device_id=self.z_peer(i)[1], device_id_type=MESH)
            return carry

        lax.fori_loop(1, self.np, plane, 0)
        lax.fori_loop(1, self.nz, column, 0)

    def wait_all(self, barrier):
        pl.semaphore_wait(barrier, self.np + self.nz - 2)

    def to_plane(self, source, target, send_sem, recv_sem):
        def step(i, carry):
            peer, device = self.plane_peer(i)
            pltpu.make_async_remote_copy(
                src_ref=source(peer),
                dst_ref=target.at[self.q],
                send_sem=send_sem,
                recv_sem=recv_sem,
                device_id=device,
                device_id_type=MESH,
            ).start()
            return carry

        lax.fori_loop(1, self.np, step, 0)

    def to_column(self, source, target, send_sem, recv_sem):
        def step(i, carry):
            peer, device = self.z_peer(i)
            pltpu.make_async_remote_copy(
                src_ref=source(peer),
                dst_ref=target.at[self.z],
                send_sem=send_sem,
                recv_sem=recv_sem,
                device_id=device,
                device_id_type=MESH,
            ).start()
            return carry

        lax.fori_loop(1, self.nz, step, 0)


def wait_bytes(buffer, count, sem):
    part = buffer.at[pl.ds(0, count)]
    pltpu.make_async_copy(part, part, sem).wait()


class Refs:
    def __init__(self, names, refs):
        for name, ref in zip(names, refs, strict=True):
            setattr(self, name, ref)


INPUTS = (
    "start",
    "q_hbm",
    "k_hbm",
    "v_hbm",
    "res_hbm",
    "op_hbm",
    "pp_hbm",
    "bias_hbm",
    "gain_hbm",
    "w_in_hbm",
    "w_out_hbm",
    "cot_hbm",
    "mask_hbm",
    "chain_hbm",
    "mask_flat_hbm",
    "chain_flat_hbm",
)
LOADS = (
    "k",
    "v",
    "pp",
    "q",
    "mask",
    "res",
    "chain",
    "bias",
    "gain",
    "w_in",
    "w_out",
    "op",
    "cot",
    "mask_flat",
    "chain_flat",
)


def pair_rows(r, i, per, columns, first):
    gain = r.gain[...]
    rows = [i * per + j for j in range(per)]
    lefts = [r.ab[pl.ds(columns + t, 1), :] for t in rows]
    right = r.ab[pl.ds(0, columns), :]
    spread = jnp.concatenate([jnp.broadcast_to(left, (E, E)) for left in lefts], axis=0)
    dots = nt(right.astype(BF), spread.astype(BF)) * (1.0 / E)
    seeds, centres = [], []
    for j, t in enumerate(rows):
        same = r.chain_column[...] == r.chain_flat[first + t].astype(F32)
        seed = lefts[j] * right + jnp.where(same, r.bias[1:2, :], r.bias[0:1, :])
        mean = dots[:, j * E : (j + 1) * E] + jnp.where(
            same, r.bias_mean[1:2, :], r.bias_mean[0:1, :]
        )
        seeds.append(seed)
        centres.append(seed - mean)
    inverses = []
    for j in range(0, per, 2):
        squares = jnp.concatenate([c * c for c in centres[j : j + 2]], axis=1).astype(BF)
        inverse = lax.rsqrt(nn(squares, r.means[...]) + 1e-05)
        inverses += [inverse[:, :E], inverse[:, E:]]
    normeds = [c * inverse for c, inverse in zip(centres, inverses)]
    scaled = jnp.concatenate([(n * gain).astype(BF) for n in normeds], axis=0)
    cots = [r.cot[t] for t in rows]
    half = nn(scaled, r.w_half[...])
    d_act = nt(jnp.concatenate(cots, axis=0), r.w_out_half[...])
    turned = jnp.tanh(half)
    raised = 1.0 + turned
    act = half * raised
    d_hidden = (d_act * (raised + act * (1.0 - turned))).astype(BF)
    y = nn(act.astype(BF), r.w_out[...])
    d_scaled = nt(d_hidden, r.w_in[...])
    total = jnp.zeros((columns, E), F32)
    for j, t in enumerate(rows):
        live = r.mask_flat[first + t].astype(F32)
        block = slice(j * columns, (j + 1) * columns)
        r.out[t] = ((seeds[j] + y[block]) * (r.live_column[...] * live)).astype(BF)
        d_normed = d_scaled[block] * gain
        both = jnp.concatenate([d_normed, d_normed * normeds[j]], axis=1).astype(BF)
        both = nn(both, r.means[...])
        d_seed = cots[j].astype(F32) + inverses[j] * (
            d_normed - both[:, :E] - normeds[j] * both[:, E:]
        )
        total = total + d_seed * (lefts[j] * live)
        r.grads[pl.ds(columns + t, 1), :] = live * jnp.sum(
            d_seed * r.right_live[...], axis=0, keepdims=True
        )
    r.grads[pl.ds(0, columns), :] += total


def kernel(sizes, names, *refs):
    r = Refs(names, refs)
    me = Place(sizes)
    nz, pr, pc, np_ = me.nz, me.pr, me.pc, me.np
    z, q = me.z, me.q
    rb = r.q.shape[0]
    fd = r.pp.shape[0]
    wz = W // nz
    columns = 8 * np_
    slab_plane = 2 * np_
    slab_tile = slab_plane // pr
    log_np = bits(np_)

    barrier = pltpu.get_barrier_semaphore()
    loads = {}
    for i, name in enumerate(LOADS):
        target = getattr(r, name)
        if name in ("k", "v"):
            target = target.at[z]
        loads[name] = pltpu.make_async_copy(getattr(r, name + "_hbm"), target, r.load_sem.at[i])
        loads[name].start()
    me.signal_all(barrier)

    loads["pp"].wait()
    row, column = grid_of(wz, W)
    piece = nt(one_hot(column == row + z * wz), r.pp[...]).astype(BF)
    row, column = grid_of(fd, W)
    piece = nn(piece, one_hot(column == row + ((fd * q) & 127))).astype(BF)
    r.ppmsg[...] = piece
    r.ppg[q] = piece
    loads["k"].wait()
    loads["v"].wait()
    me.wait_all(barrier)

    furthest = (nz // 2, nz - 1 - nz // 2)

    def ring(chain, distance, hop):
        buf = r.k if chain < 2 else r.v
        way = 1 if chain % 2 == 0 else -1
        block = lax.rem(z - way * (distance - hop) + nz, nz)
        peer = lax.rem(z + way * hop + nz, nz)
        return pltpu.make_async_remote_copy(
            src_ref=buf.at[block],
            dst_ref=buf.at[block],
            send_sem=r.ring_send.at[chain, distance - 1],
            recv_sem=r.ring_recv.at[chain, distance - 1],
            device_id=(peer, me.prow, me.pcol),
            device_id_type=MESH,
        )

    def pass_on(chain, held):
        for hop in (2, 1):
            if held + hop <= furthest[chain % 2]:
                ring(chain, held + hop, hop).start()

    for chain in range(4):
        pass_on(chain, 0)
    me.to_plane(lambda peer: r.ppmsg, r.ppg, r.send_sem.at[0], r.recv_sem.at[0])

    row, column = grid_of(8 * np_, rb)
    r.perm[...] = one_hot(column == (row & 3) * np_ + (row >> 3))
    loads["res"].wait()
    rows_twice = nt(r.perm[...], r.res[...]).astype(BF)
    both = nn(rows_twice, r.pp[...])
    row, column = grid_of(8 * np_, E)
    is_left = (row & 7) < 4
    r.presidual[...] = jnp.where(is_left, both[:, :E], both[:, E:])
    loads["q"].wait()
    loads["mask"].wait()

    scale = 1.0 / math.sqrt(E)

    def score(block):
        raw = nt(r.q[...], r.k[block]) * scale
        live = r.mask[pl.ds(block, 1), :]
        r.scores[block] = jnp.where(live > 0, raw, -1e30)

    score(z)

    def arrive(chain, distance):
        if distance <= furthest[chain % 2]:
            ring(chain, distance, 1 if distance % 2 else 2).wait_recv()
            if distance % 2 == 0:
                pass_on(chain, distance)

    def score_at(distance):
        if distance <= furthest[0]:
            score(lax.rem(z - distance + nz, nz))
        if distance <= furthest[1]:
            score(lax.rem(z + distance, nz))

    w0 = r.start[0] + z * slab_plane
    r0 = w0 + ((q - w0) & (np_ - 1))
    k0 = r0 >> log_np
    first = w0 + me.prow * slab_tile
    second_half = jnp.where(me.prow >= pr // 2, 1, 0)

    def make_w2():
        loads["op"].wait()
        wait_bytes(r.ppg, np_ - 1, r.recv_sem.at[0])
        total = jnp.zeros((E, wz), F32)
        for chunk in range(np_):
            at = ((fd * chunk) >> 7) << 7
            total = total + nt(r.op[:, at : at + W], r.ppg[chunk])
        row, column = grid_of(wz, wz)
        turned = nt(one_hot(row == column), total.astype(BF)).astype(BF)
        r.w2msg[...] = turned
        r.w2g[z] = turned
        me.to_column(lambda peer: r.w2msg, r.w2g, r.send_sem.at[1], r.recv_sem.at[1])

    def make_picks():
        row, column = grid_of(pc * 16, 8 * nz)
        sub = row & 15
        right_hit = (sub < 8) & (column == (2 * (row >> 4) + (sub >> 2)) * 8 + 4 + (sub & 3))
        kk = k0 + (sub - 8)
        left_hit = ((sub == 8) | (sub == 9)) & (column == (kk >> 2) * 8 + (kk & 3))
        r.pick[...] = one_hot(right_hit | left_hit)
        row, column = grid_of(columns + slab_tile, 16 * np_)
        right_hit = (row < columns) & (column == (row & (np_ - 1)) * 16 + (row >> log_np))
        left_hit = (row >= columns) & (
            column == ((first + row - columns) & (np_ - 1)) * 16 + 8 + second_half
        )
        r.place_rows[...] = one_hot(right_hit | left_hit)
        row, column = grid_of(16 * np_, columns + slab_tile)
        sub = row & 15
        owner = row >> 4
        right_hit = (sub < 8) & (column == sub * np_ + owner)
        left_hit = (
            (sub == 8 + second_half)
            & (column >= columns)
            & (((first + column - columns) & (np_ - 1)) == owner)
        )
        r.spread_rows[...] = one_hot(right_hit | left_hit)

    def make_pair_constants():
        for name in ("chain", "bias", "gain", "w_in", "w_out", "mask_flat", "chain_flat"):
            loads[name].wait()
        r.w_half[...] = (r.w_in[...].astype(F32) * 0.5).astype(BF)
        r.w_out_half[...] = (r.w_out[...].astype(F32) * 0.5).astype(BF)
        row, column = grid_of(2 * E, 2 * E)
        r.means[...] = jnp.where((row >> 7) == (column >> 7), 1.0 / E, 0.0).astype(BF)
        r.bias_mean[...] = jnp.broadcast_to(jnp.mean(r.bias[...], axis=1, keepdims=True), (2, E))
        row, column = grid_of(rb, rb)
        unit = one_hot(row == column)
        for half in range(2):
            at = pl.ds(2 * me.pcol + half, 1)
            to = pl.ds(half * rb, rb)
            for source, target in ((r.mask, r.live_column), (r.chain, r.chain_column)):
                lanes = jnp.broadcast_to(source[at, :].astype(F32), (E, rb)).astype(BF)
                target[to, :] = nt(unit, lanes)

    for distance in range(2, nz // 2 + 1, 2):
        for chain in range(4):
            arrive(chain, distance)
        if distance == 2:
            make_w2()
        if distance == 4 or nz // 2 < 4:
            make_picks()
        if distance == 6 or nz // 2 < 6:
            make_pair_constants()
        if distance < nz // 2:
            for near in (distance - 1, distance):
                for chain in range(2):
                    if near % 2:
                        arrive(chain, near)
                score_at(near)
    last = nz // 2
    for chain in range(2):
        arrive(chain, last - 1)
    score_at(last - 1)
    score_at(last)

    top = r.scores[0]
    for b in range(1, nz):
        top = jnp.maximum(top, r.scores[b])
    top = jnp.max(top, axis=1, keepdims=True)
    for distance in range(1, last + 1, 2):
        for chain in (2, 3):
            arrive(chain, distance)
    below = jnp.zeros((rb, rb), F32)
    above = jnp.zeros((rb, E), F32)
    for b in range(0, nz, 2):
        shifted = [jnp.exp(r.scores[b + i] - top) for i in range(2)]
        below = below + shifted[0] + shifted[1]
        weights = jnp.concatenate(shifted, axis=1).astype(BF)
        above = above + nn(weights, r.v[pl.ds(b, 2)].reshape(2 * rb, E))
    attended = (above / jnp.sum(below, axis=1, keepdims=True)).astype(BF)

    twice = nn(r.perm[...], attended).astype(BF)
    wait_bytes(r.w2g, nz - 1, r.recv_sem.at[1])
    both = nt(twice, r.w2g[...].reshape(W, E))
    terms = jnp.where(is_left, both[:, :E], both[:, E:]) + r.presidual[...]
    r.pmsg[...] = terms.reshape(np_, 8, E)
    me.to_plane(lambda peer: r.pmsg.at[peer], r.pbuf, r.send_sem.at[2], r.recv_sem.at[2])
    r.pbuf[q] = r.pmsg[q]
    wait_bytes(r.pbuf, np_ - 1, r.recv_sem.at[2])
    projected = jnp.sum(r.pbuf[...], axis=0).astype(BF).astype(F32)
    r.tmsg[...] = projected
    r.zbuf[z] = projected
    me.to_column(lambda peer: r.tmsg, r.zbuf, r.send_sem.at[3], r.recv_sem.at[3])
    wait_bytes(r.zbuf, nz - 1, r.recv_sem.at[3])
    chosen = nn(r.pick[...], r.zbuf[...].reshape(8 * nz, E).astype(BF)).astype(BF)
    r.msg[...] = chosen.reshape(pc, 16, E)
    me.to_plane(
        lambda peer: r.msg.at[lax.rem(peer, pc)], r.rbuf, r.send_sem.at[4], r.recv_sem.at[4]
    )
    r.rbuf[q] = r.msg[me.pcol]
    loads["cot"].wait()
    wait_bytes(r.rbuf, np_ - 1, r.recv_sem.at[4])
    r.ab[...] = nn(r.place_rows[...], r.rbuf[...].reshape(16 * np_, E))

    r.right_live[...] = r.ab[pl.ds(0, columns), :] * r.live_column[...]
    r.grads[...] = jnp.zeros_like(r.grads)
    per = min(PER, slab_tile)

    def store(i):
        part = pl.ds(i * per, per)
        return pltpu.make_async_copy(r.out.at[part], r.out_hbm.at[part], r.store_sem)

    def pair_step(i, carry):
        pair_rows(r, i, per, columns, first)
        store(i).start()
        return carry

    lax.fori_loop(0, slab_tile // per, pair_step, 0)

    r.grads[pl.ds(0, columns), :] = r.grads[pl.ds(0, columns), :] * r.live_column[...]
    gathered = nn(r.spread_rows[...], r.grads[...].astype(BF)).astype(BF)
    r.gmsg[...] = gathered.reshape(np_, 16, E)
    me.to_plane(lambda peer: r.gmsg.at[peer], r.gbuf, r.send_sem.at[5], r.recv_sem.at[5])
    r.gbuf[q] = r.gmsg[q]
    wait_bytes(r.gbuf, np_ - 1, r.recv_sem.at[5])
    by_column = jnp.sum(r.gbuf[...].astype(F32).reshape(pr, pc, 16, E), axis=0)
    over_columns = jnp.sum(by_column, axis=0)
    left0 = over_columns[8:9, :]
    left1 = over_columns[9:10, :]
    sub, _ = grid_of(8, E)
    for other in range(nz):
        k = 4 * other + (sub & 3)
        lefts = jnp.where(k == k0, left0, jnp.where(k == k0 + 1, left1, 0.0))
        r.zmsg[other] = jnp.where((sub >> 2) == other % 2, by_column[other // 2, 0:8, :], lefts)
    me.to_column(lambda peer: r.zmsg.at[peer], r.hbuf, r.send_sem.at[6], r.recv_sem.at[6])
    r.hbuf[z] = r.zmsg[z]
    wait_bytes(r.hbuf, nz - 1, r.recv_sem.at[6])
    tile = jnp.sum(r.hbuf[...], axis=0).astype(BF).astype(F32)
    r.fmsg[...] = tile
    r.fbuf[q] = tile
    me.to_plane(lambda peer: r.fmsg, r.fbuf, r.send_sem.at[7], r.recv_sem.at[7])
    odd = z & 1
    row, column = grid_of(rb, 8 * np_)
    base = (row & (np_ - 1)) * 8 + (row >> log_np)
    left_pick = one_hot(column == base + 4 * (1 - odd))
    right_pick = one_hot(column == base + 4 * odd)
    for chain in range(4):
        for distance in range(1, furthest[chain % 2] + 1):
            ring(chain, distance, 1 if distance % 2 else 2).wait_send()
    wait_bytes(r.ppg, np_ - 1, r.send_sem.at[0])
    wait_bytes(r.w2g, nz - 1, r.send_sem.at[1])
    wait_bytes(r.pbuf, np_ - 1, r.send_sem.at[2])
    wait_bytes(r.zbuf, nz - 1, r.send_sem.at[3])
    wait_bytes(r.rbuf, np_ - 1, r.send_sem.at[4])
    wait_bytes(r.gbuf, np_ - 1, r.send_sem.at[5])
    wait_bytes(r.hbuf, nz - 1, r.send_sem.at[6])
    pltpu.make_async_copy(r.out, r.out_hbm, r.store_sem).wait()
    wait_bytes(r.fbuf, np_ - 1, r.recv_sem.at[7])
    tiles = r.fbuf[...].reshape(8 * np_, E).astype(BF)
    left = nn(left_pick, tiles).astype(BF)
    right = nn(right_pick, tiles).astype(BF)
    r.lm[...] = (nt(r.pp[:, :E], left) + nt(r.pp[:, E:], right)).astype(BF)
    wait_bytes(r.fbuf, np_ - 1, r.send_sem.at[7])


PER = 8


def fused(sizes, start, operands):
    nz, pr, pc = sizes
    np_ = pr * pc
    q, k, v, res, op, pp, bias, gain, w_in, w_out, cot, mask, chain, mask_flat, chain_flat = operands
    rb = q.shape[0]
    columns = 8 * np_
    tile = 2 * np_ // pr
    wz = W // nz
    vmem, dma = pltpu.VMEM, pltpu.SemaphoreType.DMA
    steps = max(1, nz // 2)
    scratch = {
        "q": vmem(q.shape, BF),
        "k": vmem((nz, rb, E), BF),
        "v": vmem((nz, rb, E), BF),
        "res": vmem(res.shape, BF),
        "op": vmem(op.shape, BF),
        "pp": vmem(pp.shape, BF),
        "bias": vmem(bias.shape, F32),
        "gain": vmem(gain.shape, F32),
        "w_in": vmem(w_in.shape, BF),
        "w_out": vmem(w_out.shape, BF),
        "cot": vmem(cot.shape, BF),
        "mask": vmem(mask.shape, jnp.int32),
        "chain": vmem(chain.shape, jnp.int32),
        "mask_flat": pltpu.SMEM(mask_flat.shape, jnp.int32),
        "chain_flat": pltpu.SMEM(chain_flat.shape, jnp.int32),
        "scores": vmem((nz, rb, rb), F32),
        "perm": vmem((8 * np_, rb), BF),
        "pick": vmem((pc * 16, 8 * nz), BF),
        "place_rows": vmem((columns + tile, 16 * np_), BF),
        "spread_rows": vmem((16 * np_, columns + tile), BF),
        "presidual": vmem((8 * np_, E), F32),
        "ppmsg": vmem((wz, W), BF),
        "ppg": vmem((np_, wz, W), BF),
        "w2msg": vmem((wz, E), BF),
        "w2g": vmem((nz, wz, E), BF),
        "pmsg": vmem((np_, 8, E), F32),
        "pbuf": vmem((np_, 8, E), F32),
        "tmsg": vmem((8, E), F32),
        "zbuf": vmem((nz, 8, E), F32),
        "msg": vmem((pc, 16, E), BF),
        "rbuf": vmem((np_, 16, E), BF),
        "ab": vmem((columns + tile, E), F32),
        "w_half": vmem(w_in.shape, BF),
        "w_out_half": vmem(w_out.shape, BF),
        "means": vmem((2 * E, 2 * E), BF),
        "bias_mean": vmem((2, E), F32),
        "live_column": vmem((columns, E), F32),
        "chain_column": vmem((columns, E), F32),
        "right_live": vmem((columns, E), F32),
        "out": vmem(cot.shape, BF),
        "grads": vmem((columns + tile, E), F32),
        "gmsg": vmem((np_, 16, E), BF),
        "gbuf": vmem((np_, 16, E), BF),
        "zmsg": vmem((nz, 8, E), F32),
        "hbuf": vmem((nz, 8, E), F32),
        "fmsg": vmem((8, E), F32),
        "fbuf": vmem((np_, 8, E), F32),
        "load_sem": dma((len(LOADS),)),
        "store_sem": dma,
        "ring_send": dma((4, steps)),
        "ring_recv": dma((4, steps)),
        "send_sem": dma((8,)),
        "recv_sem": dma((8,)),
    }
    hbm = pl.BlockSpec(memory_space=pltpu.HBM)
    return pl.pallas_call(
        functools.partial(kernel, sizes, INPUTS + ("out_hbm", "lm") + tuple(scratch)),
        out_shape=(
            jax.ShapeDtypeStruct(cot.shape, BF),
            jax.ShapeDtypeStruct((pp.shape[0], rb), BF),
        ),
        in_specs=[pl.BlockSpec(memory_space=pltpu.SMEM)] + [hbm] * len(operands),
        out_specs=(hbm, pl.BlockSpec(memory_space=pltpu.VMEM)),
        scratch_shapes=list(scratch.values()),
        compiler_params=pltpu.CompilerParams(
            collective_id=0, has_side_effects=True, vmem_limit_bytes=56 << 20
        ),
        name="attend_pair_and_gradient",
    )(start, *operands)


def body(
    sizes,
    queries,
    keys,
    values,
    residual,
    out_proj,
    pair_proj,
    chain_bias,
    ln_gain,
    w_in,
    w_out,
    pair_cot,
    residue_mask,
    chain_ids,
    slab_start,
):
    nz, rb = sizes[0], queries.shape[0]
    operands = (
        queries,
        keys,
        values,
        residual.T,
        out_proj,
        pair_proj,
        chain_bias,
        ln_gain.reshape(1, E),
        w_in,
        w_out,
        pair_cot,
        residue_mask.reshape(nz, rb),
        chain_ids.reshape(nz, rb),
        residue_mask,
        chain_ids,
    )
    pair_out, lm_grad = fused(sizes, slab_start, operands)
    return pair_out, lm_grad.T


def solution(mesh):
    sizes = tuple(mesh.shape[name] for name in ("lm", "prow", "pcol"))
    return jax.shard_map(
        functools.partial(body, sizes),
        mesh=mesh,
        in_specs=(
            P("lm", ("prow", "pcol")),
            P("lm", ("prow", "pcol")),
            P("lm", ("prow", "pcol")),
            P("lm", ("prow", "pcol")),
            P(("prow", "pcol"), None),
            P(("prow", "pcol"), None),
            P(),
            P(),
            P(),
            P(),
            P(("lm", "prow"), "pcol", None),
            P(),
            P(),
            P(),
        ),
        out_specs=(P(("lm", "prow"), "pcol", None), P("lm", ("prow", "pcol"))),
        check_vma=False,
    )
```

time: 583 us -> 91.8 us (0.16)
  waiting for transfers between devices: 343 us -> 0 us
  blocking collectives: 175 us -> 0 us
  Pallas kernels: 0 us -> 87.4 us
  other arithmetic: 24.9 us -> 0 us
  matrix products: 20.9 us -> 0 us
  between operations: 14.7 us -> 1.3 us
    reduce_scatter x1 -> x0, waiting for transfers between devices: 158 us -> none  [body(): lax.psum_scatter(lax.dot_general(out_proj, attended, (((0,), (1,)), ((),...]
    psum x1 -> x0, waiting for transfers between devices: 126 us -> none  [body(): projected_here = lax.psum(proj_terms.astype(jnp.bfloat16), ('prow', 'pcol'))]
    psum x1 -> x0, blocking collectives: 121 us -> none  [body(): summed_all = lax.psum(local, ('lm', 'prow', 'pcol'))]
    pallas_call x0 -> x1, Pallas kernels: none -> 87.4 us  [fused(): pl.pallas_call(functools.partial(kernel, sizes, INPUTS + ('out_hbm', 'lm'...]
    all_gather x1 -> x0, waiting for transfers between devices: 58.5 us -> none  [body(): projected = lax.all_gather(projected_here, 'lm', axis=0, tiled=True)]
    all_gather x2 -> x0, blocking collectives: 54.2 us -> none  [the longest x1 32 us: body(): key_piece = lax.all_gather(keys, 'lm', axis=0, tiled=True)]
    dot_general x7 -> x0, matrix products: 20.9 us -> none  [the longest x1 9.35 us: pair_terms(): lax.dot_general(d_hidden, w_in, (((1,), (1,)), ((), ())), preferred_eleme...]
    reduce_sum x4 -> x0, other arithmetic: 14.4 us -> none  [the longest x1 8.96 us: pair_terms(): grad_columns = jnp.sum(d_prod * a_float[:, None, :], axis=0)]
  transfers between devices with their start and end apart: 3 -> 0, of which waited for: 3 -> 0; matrix products, arithmetic and copies ran while one was open for 1% -> 0% of each run, Pallas kernels for 0% -> 0%
where the time goes in v2:
time: 91.8 us; the launch traced here: 91.6 us
  Pallas kernels  87.4 us (95%)
  local copies, waits for them, and re-layouts  2.93 us (3%)
  between operations  1.3 us (1%)
    pallas_call x1, Pallas kernels, fused(): pl.pallas_call(functools.partial(kernel, sizes, INPUTS + ('out_hbm', 'lm'...  87.4 us
    unnamed x4, local copies, waits for them, and re-layouts  2.93 us

profile of v2, /device:TPU:1, one launch (start us, length us, event | category | flops | bytes accessed | tf_op | source)
XLA Modules:
  0.0 91.6 jit_solution(11317837046469153269)
XLA Ops:
  1.3 87.4 %attend_pair_and_gradient.1 = (bf16[16,256,128]{2,1,0:T(8,128)(2,1)}, bf16[160,128]{1,0:T(8,128)(2,1)}) custom-call(s32[1]{0:T(128)S(6)} %copy.18.refs_0_, bf16[128,128]{1,0:T(8,128)(2,1)} %refs_1_.1, bf16[128,128]{1,0:T(8,128)(2,1)} %refs_2_.1, bf16[128,128]{1,0:T(8,128)(2,1)} %refs_3_.1, bf16[160,128]{1,0:T(8,128)(2,1)} %bitcast.6, ...), custom_call_target="tpu_custom_call" | custom-call | tf_op jit(solution)/shard_map/attend_pair_and_gradient/pallas_call | solution.py:544
  88.7 0.0 copy-start
  88.7 2.3 %copy.19 = bf16[16,256,128]{2,1,0:T(8,128)(2,1)} copy(bf16[16,256,128]{2,1,0:T(8,128)(2,1)} %get-tuple-element.8) | data formatting | bytes 2097152
  91.0 0.0 copy-done
  91.0 0.6 copy.20
Async XLA Ops:
  88.7 2.3 %copy-start = (bf16[160,128]{1,0:T(8,128)(2,1)S(1)}, bf16[160,128]{1,0:T(8,128)(2,1)}, u32[]{:S(2)}) copy-start(bf16[160,128]{1,0:T(8,128)(2,1)} %get-tuple-element.5) | copy-start | bytes 122884

commit v3 on v2

--- a/solution.py
+++ b/solution.py
@@ -35,6 +35,22 @@
 
 def bits(n):
     return n.bit_length() - 1
+
+
+def plane_order(pr, pc):
+    offsets = list(range(1, pr * pc))
+    if (pr, pc) != (4, 8):
+        return offsets
+    ring = (0, 1, 2, 1)
+
+    def hops(m):
+        return ring[(m >> 1) & 3] + ring[((m & 1) << 1) | (m >> 4)]
+
+    return sorted(offsets, key=lambda m: -hops(m))
+
+
+def z_order(nz):
+    return sorted(range(1, nz), key=lambda i: -min(i, nz - i))
 
 
 class Place:
@@ -46,60 +62,47 @@
         self.pcol = lax.axis_index("pcol")
         self.q = self.prow * self.pc + self.pcol
 
-    def plane_peer(self, i):
-        peer = lax.rem(self.q + i, self.np)
-        return peer, (self.z, peer // self.pc, lax.rem(peer, self.pc))
+    def plane_peer(self, m):
+        prow = lax.bitwise_xor(self.prow, m // self.pc)
+        pcol = lax.bitwise_xor(self.pcol, m % self.pc)
+        return lax.bitwise_xor(self.q, m), (self.z, prow, pcol)
 
     def z_peer(self, i):
         peer = lax.rem(self.z + i, self.nz)
         return peer, (peer, self.prow, self.pcol)
 
+    def peers(self):
+        for i in z_order(self.nz):
+            yield self.z_peer(i)[1]
+        for m in plane_order(self.pr, self.pc):
+            yield self.plane_peer(m)[1]
+
     def signal_all(self, barrier):
-        def plane(i, carry):
-            pl.semaphore_signal(
-                barrier, inc=1, device_id=self.plane_peer(i)[1], device_id_type=MESH
-            )
-            return carry
-
-        def column(i, carry):
-            pl.semaphore_signal(barrier, inc=1, device_id=self.z_peer(i)[1], device_id_type=MESH)
-            return carry
-
-        lax.fori_loop(1, self.np, plane, 0)
-        lax.fori_loop(1, self.nz, column, 0)
+        for device in self.peers():
+            pl.semaphore_signal(barrier, inc=1, device_id=device, device_id_type=MESH)
 
     def wait_all(self, barrier):
         pl.semaphore_wait(barrier, self.np + self.nz - 2)
 
+    def send(self, source, target, send_sem, recv_sem, device):
+        pltpu.make_async_remote_copy(
+            src_ref=source,
+            dst_ref=target,
+            send_sem=send_sem,
+            recv_sem=recv_sem,
+            device_id=device,
+            device_id_type=MESH,
+        ).start()
+
     def to_plane(self, source, target, send_sem, recv_sem):
-        def step(i, carry):
-            peer, device = self.plane_peer(i)
-            pltpu.make_async_remote_copy(
-                src_ref=source(peer),
-                dst_ref=target.at[self.q],
-                send_sem=send_sem,
-                recv_sem=recv_sem,
-                device_id=device,
-                device_id_type=MESH,
-            ).start()
-            return carry
-
-        lax.fori_loop(1, self.np, step, 0)
+        for m in plane_order(self.pr, self.pc):
+            peer, device = self.plane_peer(m)
+            self.send(source(peer), target.at[self.q], send_sem, recv_sem, device)
 
     def to_column(self, source, target, send_sem, recv_sem):
-        def step(i, carry):
+        for i in z_order(self.nz):
             peer, device = self.z_peer(i)
-            pltpu.make_async_remote_copy(
-                src_ref=source(peer),
-                dst_ref=target.at[self.z],
-                send_sem=send_sem,
-                recv_sem=recv_sem,
-                device_id=device,
-                device_id_type=MESH,
-            ).start()
-            return carry
-
-        lax.fori_loop(1, self.nz, step, 0)
+            self.send(source(peer), target.at[self.z], send_sem, recv_sem, device)
 
 
 def wait_bytes(buffer, count, sem):
@@ -150,54 +153,80 @@
 )
 
 
-def pair_rows(r, i, per, columns, first):
-    gain = r.gain[...]
-    rows = [i * per + j for j in range(per)]
-    lefts = [r.ab[pl.ds(columns + t, 1), :] for t in rows]
-    right = r.ab[pl.ds(0, columns), :]
-    spread = jnp.concatenate([jnp.broadcast_to(left, (E, E)) for left in lefts], axis=0)
-    dots = nt(right.astype(BF), spread.astype(BF)) * (1.0 / E)
-    seeds, centres = [], []
-    for j, t in enumerate(rows):
-        same = r.chain_column[...] == r.chain_flat[first + t].astype(F32)
-        seed = lefts[j] * right + jnp.where(same, r.bias[1:2, :], r.bias[0:1, :])
-        mean = dots[:, j * E : (j + 1) * E] + jnp.where(
-            same, r.bias_mean[1:2, :], r.bias_mean[0:1, :]
-        )
-        seeds.append(seed)
-        centres.append(seed - mean)
-    inverses = []
-    for j in range(0, per, 2):
-        squares = jnp.concatenate([c * c for c in centres[j : j + 2]], axis=1).astype(BF)
-        inverse = lax.rsqrt(nn(squares, r.means[...]) + 1e-05)
-        inverses += [inverse[:, :E], inverse[:, E:]]
-    normeds = [c * inverse for c, inverse in zip(centres, inverses)]
-    scaled = jnp.concatenate([(n * gain).astype(BF) for n in normeds], axis=0)
-    cots = [r.cot[t] for t in rows]
-    half = nn(scaled, r.w_half[...])
-    d_act = nt(jnp.concatenate(cots, axis=0), r.w_out_half[...])
-    turned = jnp.tanh(half)
-    raised = 1.0 + turned
-    act = half * raised
-    d_hidden = (d_act * (raised + act * (1.0 - turned))).astype(BF)
-    y = nn(act.astype(BF), r.w_out[...])
-    d_scaled = nt(d_hidden, r.w_in[...])
+class PairGroup:
+    def __init__(self, r, rows, columns, first):
+        self.r, self.rows, self.columns, self.first = r, rows, columns, first
+
+    def norm_and_hidden(self):
+        r, rows, columns = self.r, self.rows, self.columns
+        gain = r.gain[...]
+        self.lefts = [r.ab[pl.ds(columns + t, 1), :] for t in rows]
+        right = r.ab[pl.ds(0, columns), :]
+        spread = jnp.concatenate([jnp.broadcast_to(left, (E, E)) for left in self.lefts], axis=0)
+        dots = nt(right.astype(BF), spread.astype(BF)) * (1.0 / E)
+        self.seeds, centres = [], []
+        for j, t in enumerate(rows):
+            same = r.chain_column[...] == r.chain_flat[self.first + t].astype(F32)
+            seed = self.lefts[j] * right + jnp.where(same, r.bias[1:2, :], r.bias[0:1, :])
+            mean = dots[:, j * E : (j + 1) * E] + jnp.where(
+                same, r.bias_mean[1:2, :], r.bias_mean[0:1, :]
+            )
+            self.seeds.append(seed)
+            centres.append(seed - mean)
+        self.inverses = []
+        for j in range(0, len(rows), 2):
+            squares = jnp.concatenate([c * c for c in centres[j : j + 2]], axis=1).astype(BF)
+            inverse = lax.rsqrt(nn(squares, r.means[...]) + 1e-05)
+            self.inverses += [inverse[:, :E], inverse[:, E:]]
+        self.normeds = [c * inverse for c, inverse in zip(centres, self.inverses)]
+        scaled = jnp.concatenate([(n * gain).astype(BF) for n in self.normeds], axis=0)
+        self.half = nn(scaled, r.w_half[...])
+
+    def activate(self):
+        r = self.r
+        d_act = jnp.concatenate([r.d_act[t] for t in self.rows], axis=0)
+        turned = jnp.tanh(self.half)
+        raised = 1.0 + turned
+        act = self.half * raised
+        d_hidden = (d_act * (raised + act * (1.0 - turned))).astype(BF)
+        self.y = nn(act.astype(BF), r.w_out[...])
+        self.d_scaled = nt(d_hidden, r.w_in[...])
+
+    def finish(self, total):
+        r, columns = self.r, self.columns
+        gain = r.gain[...]
+        for j, t in enumerate(self.rows):
+            live = r.mask_flat[self.first + t].astype(F32)
+            block = slice(j * columns, (j + 1) * columns)
+            r.out[t] = ((self.seeds[j] + self.y[block]) * (r.live_column[...] * live)).astype(BF)
+            d_normed = self.d_scaled[block] * gain
+            both = jnp.concatenate([d_normed, d_normed * self.normeds[j]], axis=1).astype(BF)
+            both = nn(both, r.means[...])
+            d_seed = r.cot[t].astype(F32) + self.inverses[j] * (
+                d_normed - both[:, :E] - self.normeds[j] * both[:, E:]
+            )
+            total = total + d_seed * (self.lefts[j] * live)
+            r.grads[pl.ds(columns + t, 1), :] = live * jnp.sum(
+                d_seed * r.right_live[...], axis=0, keepdims=True
+            )
+        return total
+
+
+def pair_tile(r, tile, columns, first, done):
+    per = min(4, tile)
+    groups = [
+        PairGroup(r, range(at, at + per), columns, first) for at in range(0, tile, per)
+    ]
     total = jnp.zeros((columns, E), F32)
-    for j, t in enumerate(rows):
-        live = r.mask_flat[first + t].astype(F32)
-        block = slice(j * columns, (j + 1) * columns)
-        r.out[t] = ((seeds[j] + y[block]) * (r.live_column[...] * live)).astype(BF)
-        d_normed = d_scaled[block] * gain
-        both = jnp.concatenate([d_normed, d_normed * normeds[j]], axis=1).astype(BF)
-        both = nn(both, r.means[...])
-        d_seed = cots[j].astype(F32) + inverses[j] * (
-            d_normed - both[:, :E] - normeds[j] * both[:, E:]
-        )
-        total = total + d_seed * (lefts[j] * live)
-        r.grads[pl.ds(columns + t, 1), :] = live * jnp.sum(
-            d_seed * r.right_live[...], axis=0, keepdims=True
-        )
-    r.grads[pl.ds(0, columns), :] += total
+    for i in range(len(groups) + 2):
+        if i < len(groups):
+            groups[i].norm_and_hidden()
+        if 0 <= i - 1 < len(groups):
+            groups[i - 1].activate()
+        if i >= 2:
+            total = groups[i - 2].finish(total)
+            done((i - 2) * per, per)
+    return total
 
 
 def kernel(sizes, names, *refs):
@@ -351,23 +380,35 @@
                 lanes = jnp.broadcast_to(source[at, :].astype(F32), (E, rb)).astype(BF)
                 target[to, :] = nt(unit, lanes)
 
-    for distance in range(2, nz // 2 + 1, 2):
+    def make_d_act(first_row, end_row):
+        for t in range(first_row, end_row):
+            r.d_act[t] = nt(r.cot[t], r.w_out_half[...]).astype(r.d_act.dtype)
+
+    last = nz // 2
+    third = max(1, slab_tile // 4)
+    chores = {
+        0: (make_pair_constants, make_picks),
+        2: (lambda: loads["cot"].wait(), lambda: make_d_act(0, third)),
+        4: (make_w2,),
+        6: (lambda: make_d_act(third, slab_tile),),
+    }
+    for chore in chores[0]:
+        chore()
+    for distance in range(2, last, 2):
         for chain in range(4):
             arrive(chain, distance)
-        if distance == 2:
-            make_w2()
-        if distance == 4 or nz // 2 < 4:
-            make_picks()
-        if distance == 6 or nz // 2 < 6:
-            make_pair_constants()
-        if distance < nz // 2:
-            for near in (distance - 1, distance):
+        for chore in chores.pop(distance, ()):
+            chore()
+        for near in (distance - 1, distance):
+            if near % 2:
                 for chain in range(2):
-                    if near % 2:
-                        arrive(chain, near)
-                score_at(near)
-    last = nz // 2
-    for chain in range(2):
+                    arrive(chain, near)
+            score_at(near)
+    for stage in (2, 4, 6):
+        for chore in chores.pop(stage, ()):
+            chore()
+    for chain in (0, 1):
+        arrive(chain, last)
         arrive(chain, last - 1)
     score_at(last - 1)
     score_at(last)
@@ -376,16 +417,18 @@
     for b in range(1, nz):
         top = jnp.maximum(top, r.scores[b])
     top = jnp.max(top, axis=1, keepdims=True)
-    for distance in range(1, last + 1, 2):
-        for chain in (2, 3):
-            arrive(chain, distance)
     below = jnp.zeros((rb, rb), F32)
     above = jnp.zeros((rb, E), F32)
-    for b in range(0, nz, 2):
-        shifted = [jnp.exp(r.scores[b + i] - top) for i in range(2)]
+    for distance in range(1, last + 1):
+        if distance % 2 or distance == last:
+            for chain in (2, 3):
+                arrive(chain, distance)
+        left = lax.rem(z - distance + nz, nz)
+        right = lax.rem(z + (distance if distance < last else 0), nz)
+        shifted = [jnp.exp(r.scores[b] - top) for b in (left, right)]
         below = below + shifted[0] + shifted[1]
         weights = jnp.concatenate(shifted, axis=1).astype(BF)
-        above = above + nn(weights, r.v[pl.ds(b, 2)].reshape(2 * rb, E))
+        above = above + nn(weights, jnp.concatenate([r.v[left], r.v[right]], axis=0))
     attended = (above / jnp.sum(below, axis=1, keepdims=True)).astype(BF)
 
     twice = nn(r.perm[...], attended).astype(BF)
@@ -407,26 +450,17 @@
         lambda peer: r.msg.at[lax.rem(peer, pc)], r.rbuf, r.send_sem.at[4], r.recv_sem.at[4]
     )
     r.rbuf[q] = r.msg[me.pcol]
-    loads["cot"].wait()
     wait_bytes(r.rbuf, np_ - 1, r.recv_sem.at[4])
     r.ab[...] = nn(r.place_rows[...], r.rbuf[...].reshape(16 * np_, E))
 
     r.right_live[...] = r.ab[pl.ds(0, columns), :] * r.live_column[...]
-    r.grads[...] = jnp.zeros_like(r.grads)
-    per = min(PER, slab_tile)
-
-    def store(i):
-        part = pl.ds(i * per, per)
-        return pltpu.make_async_copy(r.out.at[part], r.out_hbm.at[part], r.store_sem)
-
-    def pair_step(i, carry):
-        pair_rows(r, i, per, columns, first)
-        store(i).start()
-        return carry
-
-    lax.fori_loop(0, slab_tile // per, pair_step, 0)
-
-    r.grads[pl.ds(0, columns), :] = r.grads[pl.ds(0, columns), :] * r.live_column[...]
+
+    def store(at, count):
+        part = pl.ds(at, count)
+        pltpu.make_async_copy(r.out.at[part], r.out_hbm.at[part], r.store_sem).start()
+
+    total = pair_tile(r, slab_tile, columns, first, store)
+    r.grads[pl.ds(0, columns), :] = total * r.live_column[...]
     gathered = nn(r.spread_rows[...], r.grads[...].astype(BF)).astype(BF)
     r.gmsg[...] = gathered.reshape(np_, 16, E)
     me.to_plane(lambda peer: r.gmsg.at[peer], r.gbuf, r.send_sem.at[5], r.recv_sem.at[5])
@@ -463,16 +497,16 @@
     wait_bytes(r.rbuf, np_ - 1, r.send_sem.at[4])
     wait_bytes(r.gbuf, np_ - 1, r.send_sem.at[5])
     wait_bytes(r.hbuf, nz - 1, r.send_sem.at[6])
-    pltpu.make_async_copy(r.out, r.out_hbm, r.store_sem).wait()
     wait_bytes(r.fbuf, np_ - 1, r.recv_sem.at[7])
     tiles = r.fbuf[...].reshape(8 * np_, E).astype(BF)
+    pltpu.make_async_copy(r.out, r.out_hbm, r.store_sem).wait()
     left = nn(left_pick, tiles).astype(BF)
     right = nn(right_pick, tiles).astype(BF)
     r.lm[...] = (nt(r.pp[:, :E], left) + nt(r.pp[:, E:], right)).astype(BF)
     wait_bytes(r.fbuf, np_ - 1, r.send_sem.at[7])
 
 
-PER = 8
+D_ACT = F32
 
 
 def fused(sizes, start, operands):
@@ -518,6 +552,8 @@
         "msg": vmem((pc, 16, E), BF),
         "rbuf": vmem((np_, 16, E), BF),
         "ab": vmem((columns + tile, E), F32),
+        "out": vmem(cot.shape, BF),
+        "store_sem": dma,
         "w_half": vmem(w_in.shape, BF),
         "w_out_half": vmem(w_out.shape, BF),
         "means": vmem((2 * E, 2 * E), BF),
@@ -525,7 +561,7 @@
         "live_column": vmem((columns, E), F32),
         "chain_column": vmem((columns, E), F32),
         "right_live": vmem((columns, E), F32),
-        "out": vmem(cot.shape, BF),
+        "d_act": vmem(cot.shape[:2] + w_in.shape[1:], D_ACT),
         "grads": vmem((columns + tile, E), F32),
         "gmsg": vmem((np_, 16, E), BF),
         "gbuf": vmem((np_, 16, E), BF),
@@ -534,7 +570,6 @@
         "fmsg": vmem((8, E), F32),
         "fbuf": vmem((np_, 8, E), F32),
         "load_sem": dma((len(LOADS),)),
-        "store_sem": dma,
         "ring_send": dma((4, steps)),
         "ring_recv": dma((4, steps)),
         "send_sem": dma((8,)),
@@ -551,10 +586,35 @@
         out_specs=(hbm, pl.BlockSpec(memory_space=pltpu.VMEM)),
         scratch_shapes=list(scratch.values()),
         compiler_params=pltpu.CompilerParams(
-            collective_id=0, has_side_effects=True, vmem_limit_bytes=56 << 20
+            collective_id=0, has_side_effects=True, vmem_limit_bytes=58 << 20
         ),
         name="attend_pair_and_gradient",
     )(start, *operands)
+
+
+def store_kernel(out, lm, out_hbm, lm_hbm, sem):
+    parts = sem.shape[0] - 1
+    rows = out.shape[0] // parts
+    copies = [pltpu.make_async_copy(lm, lm_hbm, sem.at[parts])]
+    for i in range(parts):
+        part = pl.ds(i * rows, rows)
+        copies.append(pltpu.make_async_copy(out.at[part], out_hbm.at[part], sem.at[i]))
+    for copy in copies:
+        copy.start()
+    for copy in copies:
+        copy.wait()
+
+
+def store(out, lm):
+    return pl.pallas_call(
+        store_kernel,
+        out_shape=tuple(jax.ShapeDtypeStruct(a.shape, a.dtype) for a in (out, lm)),
+        in_specs=[pl.BlockSpec(memory_space=pltpu.HBM)] * 2,
+        out_specs=(pl.BlockSpec(memory_space=pltpu.HBM),) * 2,
+        scratch_shapes=[pltpu.SemaphoreType.DMA((min(8, out.shape[0]) + 1,))],
+        compiler_params=pltpu.CompilerParams(vmem_limit_bytes=62 << 20),
+        name="store_results",
+    )(out, lm)
 
 
 def body(
@@ -592,7 +652,7 @@
         residue_mask,
         chain_ids,
     )
-    pair_out, lm_grad = fused(sizes, slab_start, operands)
+    pair_out, lm_grad = store(*fused(sizes, slab_start, operands))
     return pair_out, lm_grad.T
 
 

time: 91.8 us -> 117 us (1.27)
  Pallas kernels: 87.4 us -> 115 us
  local copies, waits for them, and re-layouts: 2.93 us -> 0 us
    pallas_call x0 -> x1, Pallas kernels: none -> 34.2 us  [store(): pl.pallas_call(store_kernel, out_shape=tuple((jax.ShapeDtypeStruct(a.shap...]
    pallas_call x1, Pallas kernels: 87.4 us -> 81.2 us  [fused(): pl.pallas_call(functools.partial(kernel, sizes, INPUTS + ('out_hbm', 'lm'...]
    unnamed x4 -> x0, local copies, waits for them, and re-layouts: 2.93 us -> none
where the time goes in v3:
time: 117 us
  Pallas kernels  115 us (98%)
  between operations  1.29 us (1%)
    pallas_call x1, Pallas kernels, fused(): pl.pallas_call(functools.partial(kernel, sizes, INPUTS + ('out_hbm', 'lm'...  81.2 us
    pallas_call x1, Pallas kernels, store(): pl.pallas_call(store_kernel, out_shape=tuple((jax.ShapeDtypeStruct(a.shap...  34.2 us

profile of v3, /device:TPU:1, one launch (start us, length us, event | category | flops | bytes accessed | tf_op | source)
XLA Modules:
  0.0 116.7 jit_solution(11823235615268341414)
XLA Ops:
  1.3 81.2 %attend_pair_and_gradient.1 = (bf16[16,256,128]{2,1,0:T(8,128)(2,1)}, bf16[160,128]{1,0:T(8,128)(2,1)}) custom-call(s32[1]{0:T(128)S(6)} %copy.16.refs_0_, bf16[128,128]{1,0:T(8,128)(2,1)} %refs_1_.1, bf16[128,128]{1,0:T(8,128)(2,1)} %refs_2_.1, bf16[128,128]{1,0:T(8,128)(2,1)} %refs_3_.1, bf16[160,128]{1,0:T(8,128)(2,1)} %bitcast.5, ...), custom_call_target="tpu_custom_call" | custom-call | tf_op jit(solution)/shard_map/attend_pair_and_gradient/pallas_call | solution.py:579
  82.5 34.2 %store_results.1 = (bf16[16,256,128]{2,1,0:T(8,128)(2,1)}, bf16[160,128]{1,0:T(8,128)(2,1)}) custom-call(bf16[16,256,128]{2,1,0:T(8,128)(2,1)} %get-tuple-element.6.out, bf16[160,128]{1,0:T(8,128)(2,1)} %get-tuple-element.7.lm), custom_call_target="tpu_custom_call" | custom-call | tf_op jit(solution)/shard_map/store_results/pallas_call | solution.py:609

commit v4 on v3

--- a/solution.py
+++ b/solution.py
@@ -249,16 +249,11 @@
         if name in ("k", "v"):
             target = target.at[z]
         loads[name] = pltpu.make_async_copy(getattr(r, name + "_hbm"), target, r.load_sem.at[i])
+    for name in LOADS[:3]:
         loads[name].start()
     me.signal_all(barrier)
-
-    loads["pp"].wait()
-    row, column = grid_of(wz, W)
-    piece = nt(one_hot(column == row + z * wz), r.pp[...]).astype(BF)
-    row, column = grid_of(fd, W)
-    piece = nn(piece, one_hot(column == row + ((fd * q) & 127))).astype(BF)
-    r.ppmsg[...] = piece
-    r.ppg[q] = piece
+    for name in LOADS[3:]:
+        loads[name].start()
     loads["k"].wait()
     loads["v"].wait()
     me.wait_all(barrier)
@@ -286,6 +281,14 @@
 
     for chain in range(4):
         pass_on(chain, 0)
+
+    loads["pp"].wait()
+    row, column = grid_of(wz, W)
+    piece = nt(one_hot(column == row + z * wz), r.pp[...]).astype(BF)
+    row, column = grid_of(fd, W)
+    piece = nn(piece, one_hot(column == row + ((fd * q) & 127))).astype(BF)
+    r.ppmsg[...] = piece
+    r.ppg[q] = piece
     me.to_plane(lambda peer: r.ppmsg, r.ppg, r.send_sem.at[0], r.recv_sem.at[0])
 
     row, column = grid_of(8 * np_, rb)
@@ -592,26 +595,37 @@
     )(start, *operands)
 
 
-def store_kernel(out, lm, out_hbm, lm_hbm, sem):
-    parts = sem.shape[0] - 1
+def store_kernel(out, lm, out_hbm, lm_hbm, out_vmem, lm_vmem, load_sem, save_sem):
+    parts = load_sem.shape[0] - 1
     rows = out.shape[0] // parts
-    copies = [pltpu.make_async_copy(lm, lm_hbm, sem.at[parts])]
+    ways = [(lm, lm_vmem, lm_hbm)]
     for i in range(parts):
         part = pl.ds(i * rows, rows)
-        copies.append(pltpu.make_async_copy(out.at[part], out_hbm.at[part], sem.at[i]))
-    for copy in copies:
-        copy.start()
-    for copy in copies:
-        copy.wait()
+        ways.append((out.at[part], out_vmem.at[part], out_hbm.at[part]))
+    loads = [pltpu.make_async_copy(w[0], w[1], load_sem.at[i]) for i, w in enumerate(ways)]
+    saves = [pltpu.make_async_copy(w[1], w[2], save_sem.at[i]) for i, w in enumerate(ways)]
+    for load in loads:
+        load.start()
+    for load, save in zip(loads, saves):
+        load.wait()
+        save.start()
+    for save in saves:
+        save.wait()
 
 
 def store(out, lm):
+    parts = min(8, out.shape[0]) + 1
     return pl.pallas_call(
         store_kernel,
         out_shape=tuple(jax.ShapeDtypeStruct(a.shape, a.dtype) for a in (out, lm)),
         in_specs=[pl.BlockSpec(memory_space=pltpu.HBM)] * 2,
         out_specs=(pl.BlockSpec(memory_space=pltpu.HBM),) * 2,
-        scratch_shapes=[pltpu.SemaphoreType.DMA((min(8, out.shape[0]) + 1,))],
+        scratch_shapes=[
+            pltpu.VMEM(out.shape, out.dtype),
+            pltpu.VMEM(lm.shape, lm.dtype),
+            pltpu.SemaphoreType.DMA((parts,)),
+            pltpu.SemaphoreType.DMA((parts,)),
+        ],
         compiler_params=pltpu.CompilerParams(vmem_limit_bytes=62 << 20),
         name="store_results",
     )(out, lm)

time: 117 us -> 84.8 us (0.72)
  Pallas kernels: 115 us -> 83.3 us
    pallas_call x1, Pallas kernels: 34.2 us -> 2.12 us  [store(): pl.pallas_call(store_kernel, out_shape=tuple((jax.ShapeDtypeStruct(a.shap...]
where the time goes in v4:
time: 84.8 us; the launch traced here: 84.6 us
  Pallas kernels  83.3 us (98%)
  between operations  1.29 us (2%)
    pallas_call x1, Pallas kernels, fused(): pl.pallas_call(functools.partial(kernel, sizes, INPUTS + ('out_hbm', 'lm'...  81.2 us
    pallas_call x1, Pallas kernels, store(): pl.pallas_call(store_kernel, out_shape=tuple((jax.ShapeDtypeStruct(a.shap...  2.12 us

profile of v4, /device:TPU:1, one launch (start us, length us, event | category | flops | bytes accessed | tf_op | source)
XLA Modules:
  0.0 84.6 jit_solution(17796724950018656607)
XLA Ops:
  1.3 81.2 %attend_pair_and_gradient.1 = (bf16[16,256,128]{2,1,0:T(8,128)(2,1)}, bf16[160,128]{1,0:T(8,128)(2,1)}) custom-call(s32[1]{0:T(128)S(6)} %copy.16.refs_0_, bf16[128,128]{1,0:T(8,128)(2,1)} %refs_1_.1, bf16[128,128]{1,0:T(8,128)(2,1)} %refs_2_.1, bf16[128,128]{1,0:T(8,128)(2,1)} %refs_3_.1, bf16[160,128]{1,0:T(8,128)(2,1)} %bitcast.5, ...), custom_call_target="tpu_custom_call" | custom-call | tf_op jit(solution)/shard_map/attend_pair_and_gradient/pallas_call | solution.py:582
  82.5 2.1 %store_results.1 = (bf16[16,256,128]{2,1,0:T(8,128)(2,1)}, bf16[160,128]{1,0:T(8,128)(2,1)}) custom-call(bf16[16,256,128]{2,1,0:T(8,128)(2,1)} %get-tuple-element.6.out, bf16[160,128]{1,0:T(8,128)(2,1)} %get-tuple-element.7.lm), custom_call_target="tpu_custom_call" | custom-call | tf_op jit(solution)/shard_map/store_results/pallas_call | solution.py:618

commit v5 on v4

--- a/solution.py
+++ b/solution.py
@@ -47,6 +47,10 @@
         return ring[(m >> 1) & 3] + ring[((m & 1) << 1) | (m >> 4)]
 
     return sorted(offsets, key=lambda m: -hops(m))
+
+
+def group_of(nz):
+    return min(8, nz)
 
 
 def z_order(nz):
@@ -71,18 +75,22 @@
         peer = lax.rem(self.z + i, self.nz)
         return peer, (peer, self.prow, self.pcol)
 
-    def peers(self):
-        for i in z_order(self.nz):
+    def near(self):
+        reach = max(2, group_of(self.nz) // 2)
+        return sorted({way * d % self.nz for d in range(1, reach + 1) for way in (1, -1)} - {0})
+
+    def greeted(self):
+        for i in self.near():
             yield self.z_peer(i)[1]
         for m in plane_order(self.pr, self.pc):
             yield self.plane_peer(m)[1]
 
     def signal_all(self, barrier):
-        for device in self.peers():
+        for device in self.greeted():
             pl.semaphore_signal(barrier, inc=1, device_id=device, device_id_type=MESH)
 
     def wait_all(self, barrier):
-        pl.semaphore_wait(barrier, self.np + self.nz - 2)
+        pl.semaphore_wait(barrier, self.np - 1 + len(self.near()))
 
     def send(self, source, target, send_sem, recv_sem, device):
         pltpu.make_async_remote_copy(
@@ -98,6 +106,14 @@
         for m in plane_order(self.pr, self.pc):
             peer, device = self.plane_peer(m)
             self.send(source(peer), target.at[self.q], send_sem, recv_sem, device)
+
+    def to_group(self, source, target, send_sem, recv_sem):
+        group = group_of(self.nz)
+        slot = lax.rem(self.z, group)
+        for i in range(-(group // 2), group // 2):
+            if i:
+                device = self.z_peer(i % self.nz)[1]
+                self.send(source, target.at[slot], send_sem, recv_sem, device)
 
     def to_column(self, source, target, send_sem, recv_sem):
         for i in z_order(self.nz):
@@ -173,11 +189,9 @@
             )
             self.seeds.append(seed)
             centres.append(seed - mean)
-        self.inverses = []
-        for j in range(0, len(rows), 2):
-            squares = jnp.concatenate([c * c for c in centres[j : j + 2]], axis=1).astype(BF)
-            inverse = lax.rsqrt(nn(squares, r.means[...]) + 1e-05)
-            self.inverses += [inverse[:, :E], inverse[:, E:]]
+        self.inverses = [
+            lax.rsqrt(jnp.mean(c * c, axis=1, keepdims=True) + 1e-05) for c in centres
+        ]
         self.normeds = [c * inverse for c, inverse in zip(centres, self.inverses)]
         scaled = jnp.concatenate([(n * gain).astype(BF) for n in self.normeds], axis=0)
         self.half = nn(scaled, r.w_half[...])
@@ -185,9 +199,10 @@
     def activate(self):
         r = self.r
         d_act = jnp.concatenate([r.d_act[t] for t in self.rows], axis=0)
-        turned = jnp.tanh(self.half)
+        half = self.half.astype(D_ACT)
+        turned = jnp.tanh(half)
         raised = 1.0 + turned
-        act = self.half * raised
+        act = half * raised
         d_hidden = (d_act * (raised + act * (1.0 - turned))).astype(BF)
         self.y = nn(act.astype(BF), r.w_out[...])
         self.d_scaled = nt(d_hidden, r.w_in[...])
@@ -236,7 +251,8 @@
     z, q = me.z, me.q
     rb = r.q.shape[0]
     fd = r.pp.shape[0]
-    wz = W // nz
+    group = group_of(nz)
+    wz = W // group
     columns = 8 * np_
     slab_plane = 2 * np_
     slab_tile = slab_plane // pr
@@ -258,7 +274,7 @@
     loads["v"].wait()
     me.wait_all(barrier)
 
-    furthest = (nz // 2, nz - 1 - nz // 2)
+    furthest = (nz // 2, nz - 1 - nz // 2, nz - 1 - nz // 2, nz // 2)
 
     def ring(chain, distance, hop):
         buf = r.k if chain < 2 else r.v
@@ -276,7 +292,7 @@
 
     def pass_on(chain, held):
         for hop in (2, 1):
-            if held + hop <= furthest[chain % 2]:
+            if held + hop <= furthest[chain]:
                 ring(chain, held + hop, hop).start()
 
     for chain in range(4):
@@ -284,7 +300,7 @@
 
     loads["pp"].wait()
     row, column = grid_of(wz, W)
-    piece = nt(one_hot(column == row + z * wz), r.pp[...]).astype(BF)
+    piece = nt(one_hot(column == row + lax.rem(z, group) * wz), r.pp[...]).astype(BF)
     row, column = grid_of(fd, W)
     piece = nn(piece, one_hot(column == row + ((fd * q) & 127))).astype(BF)
     r.ppmsg[...] = piece
@@ -312,7 +328,7 @@
     score(z)
 
     def arrive(chain, distance):
-        if distance <= furthest[chain % 2]:
+        if distance <= furthest[chain]:
             ring(chain, distance, 1 if distance % 2 else 2).wait_recv()
             if distance % 2 == 0:
                 pass_on(chain, distance)
@@ -339,8 +355,8 @@
         row, column = grid_of(wz, wz)
         turned = nt(one_hot(row == column), total.astype(BF)).astype(BF)
         r.w2msg[...] = turned
-        r.w2g[z] = turned
-        me.to_column(lambda peer: r.w2msg, r.w2g, r.send_sem.at[1], r.recv_sem.at[1])
+        r.w2g[lax.rem(z, group)] = turned
+        me.to_group(r.w2msg, r.w2g, r.send_sem.at[1], r.recv_sem.at[1])
 
     def make_picks():
         row, column = grid_of(pc * 16, 8 * nz)
@@ -435,7 +451,7 @@
     attended = (above / jnp.sum(below, axis=1, keepdims=True)).astype(BF)
 
     twice = nn(r.perm[...], attended).astype(BF)
-    wait_bytes(r.w2g, nz - 1, r.recv_sem.at[1])
+    wait_bytes(r.w2g, group - 1, r.recv_sem.at[1])
     both = nt(twice, r.w2g[...].reshape(W, E))
     terms = jnp.where(is_left, both[:, :E], both[:, E:]) + r.presidual[...]
     r.pmsg[...] = terms.reshape(np_, 8, E)
@@ -491,10 +507,10 @@
     left_pick = one_hot(column == base + 4 * (1 - odd))
     right_pick = one_hot(column == base + 4 * odd)
     for chain in range(4):
-        for distance in range(1, furthest[chain % 2] + 1):
+        for distance in range(1, furthest[chain] + 1):
             ring(chain, distance, 1 if distance % 2 else 2).wait_send()
     wait_bytes(r.ppg, np_ - 1, r.send_sem.at[0])
-    wait_bytes(r.w2g, nz - 1, r.send_sem.at[1])
+    wait_bytes(r.w2g, group - 1, r.send_sem.at[1])
     wait_bytes(r.pbuf, np_ - 1, r.send_sem.at[2])
     wait_bytes(r.zbuf, nz - 1, r.send_sem.at[3])
     wait_bytes(r.rbuf, np_ - 1, r.send_sem.at[4])
@@ -509,7 +525,7 @@
     wait_bytes(r.fbuf, np_ - 1, r.send_sem.at[7])
 
 
-D_ACT = F32
+D_ACT = BF
 
 
 def fused(sizes, start, operands):
@@ -519,7 +535,8 @@
     rb = q.shape[0]
     columns = 8 * np_
     tile = 2 * np_ // pr
-    wz = W // nz
+    group = group_of(nz)
+    wz = W // group
     vmem, dma = pltpu.VMEM, pltpu.SemaphoreType.DMA
     steps = max(1, nz // 2)
     scratch = {
@@ -547,7 +564,7 @@
         "ppmsg": vmem((wz, W), BF),
         "ppg": vmem((np_, wz, W), BF),
         "w2msg": vmem((wz, E), BF),
-        "w2g": vmem((nz, wz, E), BF),
+        "w2g": vmem((group, wz, E), BF),
         "pmsg": vmem((np_, 8, E), F32),
         "pbuf": vmem((np_, 8, E), F32),
         "tmsg": vmem((8, E), F32),

time: 84.8 us -> 81.1 us (0.956)
  Pallas kernels: 83.3 us -> 79.6 us
    pallas_call x1, Pallas kernels: 81.2 us -> 77.5 us  [fused(): pl.pallas_call(functools.partial(kernel, sizes, INPUTS + ('out_hbm', 'lm'...]
where the time goes in v5:
time: 81.1 us; the launch traced here: 80.9 us
  Pallas kernels  79.6 us (98%)
  between operations  1.29 us (2%)
    pallas_call x1, Pallas kernels, fused(): pl.pallas_call(functools.partial(kernel, sizes, INPUTS + ('out_hbm', 'lm'...  77.5 us
    pallas_call x1, Pallas kernels, store(): pl.pallas_call(store_kernel, out_shape=tuple((jax.ShapeDtypeStruct(a.shap...  2.12 us

profile of v5, /device:TPU:1, one launch (start us, length us, event | category | flops | bytes accessed | tf_op | source)
XLA Modules:
  0.0 80.9 jit_solution(16939979203588784833)
XLA Ops:
  1.3 77.5 %attend_pair_and_gradient.1 = (bf16[16,256,128]{2,1,0:T(8,128)(2,1)}, bf16[160,128]{1,0:T(8,128)(2,1)}) custom-call(s32[1]{0:T(128)S(6)} %copy.16.refs_0_, bf16[128,128]{1,0:T(8,128)(2,1)} %refs_1_.1, bf16[128,128]{1,0:T(8,128)(2,1)} %refs_2_.1, bf16[128,128]{1,0:T(8,128)(2,1)} %refs_3_.1, bf16[160,128]{1,0:T(8,128)(2,1)} %bitcast.5, ...), custom_call_target="tpu_custom_call" | custom-call | tf_op jit(solution)/shard_map/attend_pair_and_gradient/pallas_call | solution.py:599
  78.8 2.1 %store_results.1 = (bf16[16,256,128]{2,1,0:T(8,128)(2,1)}, bf16[160,128]{1,0:T(8,128)(2,1)}) custom-call(bf16[16,256,128]{2,1,0:T(8,128)(2,1)} %get-tuple-element.6.out, bf16[160,128]{1,0:T(8,128)(2,1)} %get-tuple-element.7.lm), custom_call_target="tpu_custom_call" | custom-call | tf_op jit(solution)/shard_map/store_results/pallas_call | solution.py:635

commit v6 on v5

--- a/solution.py
+++ b/solution.py
@@ -180,14 +180,13 @@
         right = r.ab[pl.ds(0, columns), :]
         spread = jnp.concatenate([jnp.broadcast_to(left, (E, E)) for left in self.lefts], axis=0)
         dots = nt(right.astype(BF), spread.astype(BF)) * (1.0 / E)
-        self.seeds, centres = [], []
+        centres = []
         for j, t in enumerate(rows):
             same = r.chain_column[...] == r.chain_flat[self.first + t].astype(F32)
             seed = self.lefts[j] * right + jnp.where(same, r.bias[1:2, :], r.bias[0:1, :])
             mean = dots[:, j * E : (j + 1) * E] + jnp.where(
                 same, r.bias_mean[1:2, :], r.bias_mean[0:1, :]
             )
-            self.seeds.append(seed)
             centres.append(seed - mean)
         self.inverses = [
             lax.rsqrt(jnp.mean(c * c, axis=1, keepdims=True) + 1e-05) for c in centres
@@ -204,7 +203,9 @@
         raised = 1.0 + turned
         act = half * raised
         d_hidden = (d_act * (raised + act * (1.0 - turned))).astype(BF)
-        self.y = nn(act.astype(BF), r.w_out[...])
+        act = act.astype(BF)
+        for j, t in enumerate(self.rows):
+            r.act[t] = act[j * self.columns : (j + 1) * self.columns]
         self.d_scaled = nt(d_hidden, r.w_in[...])
 
     def finish(self, total):
@@ -213,7 +214,6 @@
         for j, t in enumerate(self.rows):
             live = r.mask_flat[self.first + t].astype(F32)
             block = slice(j * columns, (j + 1) * columns)
-            r.out[t] = ((self.seeds[j] + self.y[block]) * (r.live_column[...] * live)).astype(BF)
             d_normed = self.d_scaled[block] * gain
             both = jnp.concatenate([d_normed, d_normed * self.normeds[j]], axis=1).astype(BF)
             both = nn(both, r.means[...])
@@ -227,7 +227,7 @@
         return total
 
 
-def pair_tile(r, tile, columns, first, done):
+def pair_tile(r, tile, columns, first):
     per = min(4, tile)
     groups = [
         PairGroup(r, range(at, at + per), columns, first) for at in range(0, tile, per)
@@ -240,8 +240,19 @@
             groups[i - 1].activate()
         if i >= 2:
             total = groups[i - 2].finish(total)
-            done((i - 2) * per, per)
     return total
+
+
+def pair_results(r, tile, columns, first):
+    right = r.ab[pl.ds(0, columns), :]
+    for t in range(tile):
+        same = r.chain_column[...] == r.chain_flat[first + t].astype(F32)
+        live = r.mask_flat[first + t].astype(F32)
+        seed = r.ab[pl.ds(columns + t, 1), :] * right + jnp.where(
+            same, r.bias[1:2, :], r.bias[0:1, :]
+        )
+        y = nn(r.act[t], r.w_out[...])
+        r.out[t] = ((seed + y) * (r.live_column[...] * live)).astype(BF)
 
 
 def kernel(sizes, names, *refs):
@@ -270,8 +281,6 @@
     me.signal_all(barrier)
     for name in LOADS[3:]:
         loads[name].start()
-    loads["k"].wait()
-    loads["v"].wait()
     me.wait_all(barrier)
 
     furthest = (nz // 2, nz - 1 - nz // 2, nz - 1 - nz // 2, nz // 2)
@@ -281,8 +290,9 @@
         way = 1 if chain % 2 == 0 else -1
         block = lax.rem(z - way * (distance - hop) + nz, nz)
         peer = lax.rem(z + way * hop + nz, nz)
+        own = r.k_hbm if chain < 2 else r.v_hbm
         return pltpu.make_async_remote_copy(
-            src_ref=buf.at[block],
+            src_ref=own if distance == hop else buf.at[block],
             dst_ref=buf.at[block],
             send_sem=r.ring_send.at[chain, distance - 1],
             recv_sem=r.ring_recv.at[chain, distance - 1],
@@ -315,13 +325,14 @@
     row, column = grid_of(8 * np_, E)
     is_left = (row & 7) < 4
     r.presidual[...] = jnp.where(is_left, both[:, :E], both[:, E:])
-    loads["q"].wait()
-    loads["mask"].wait()
+    for name in ("q", "k", "v", "mask"):
+        loads[name].wait()
+    r.q_twice[...] = nn(r.perm[...], r.q[...]).astype(BF)
 
     scale = 1.0 / math.sqrt(E)
 
     def score(block):
-        raw = nt(r.q[...], r.k[block]) * scale
+        raw = nt(r.q_twice[...], r.k[block]) * scale
         live = r.mask[pl.ds(block, 1), :]
         r.scores[block] = jnp.where(live > 0, raw, -1e30)
 
@@ -436,23 +447,26 @@
     for b in range(1, nz):
         top = jnp.maximum(top, r.scores[b])
     top = jnp.max(top, axis=1, keepdims=True)
-    below = jnp.zeros((rb, rb), F32)
-    above = jnp.zeros((rb, E), F32)
+    def pair_of(distance):
+        left = lax.rem(z - distance + nz, nz)
+        return left, lax.rem(z + (distance if distance < last else 0), nz)
+
+    below = jnp.zeros((8 * np_, rb), F32)
+    for distance in range(1, last + 1):
+        shifted = [jnp.exp(r.scores[b] - top) for b in pair_of(distance)]
+        below = below + shifted[0] + shifted[1]
+        r.weights[distance - 1] = jnp.concatenate(shifted, axis=1).astype(BF)
+    below = 1.0 / jnp.sum(below, axis=1, keepdims=True)
+    above = jnp.zeros((8 * np_, E), F32)
     for distance in range(1, last + 1):
         if distance % 2 or distance == last:
             for chain in (2, 3):
                 arrive(chain, distance)
-        left = lax.rem(z - distance + nz, nz)
-        right = lax.rem(z + (distance if distance < last else 0), nz)
-        shifted = [jnp.exp(r.scores[b] - top) for b in (left, right)]
-        below = below + shifted[0] + shifted[1]
-        weights = jnp.concatenate(shifted, axis=1).astype(BF)
-        above = above + nn(weights, jnp.concatenate([r.v[left], r.v[right]], axis=0))
-    attended = (above / jnp.sum(below, axis=1, keepdims=True)).astype(BF)
-
-    twice = nn(r.perm[...], attended).astype(BF)
+        both = jnp.concatenate([r.v[b] for b in pair_of(distance)], axis=0)
+        above = above + nn(r.weights[distance - 1], both)
+    attended = (above * below).astype(BF)
     wait_bytes(r.w2g, group - 1, r.recv_sem.at[1])
-    both = nt(twice, r.w2g[...].reshape(W, E))
+    both = nt(attended, r.w2g[...].reshape(W, E))
     terms = jnp.where(is_left, both[:, :E], both[:, E:]) + r.presidual[...]
     r.pmsg[...] = terms.reshape(np_, 8, E)
     me.to_plane(lambda peer: r.pmsg.at[peer], r.pbuf, r.send_sem.at[2], r.recv_sem.at[2])
@@ -474,16 +488,15 @@
 
     r.right_live[...] = r.ab[pl.ds(0, columns), :] * r.live_column[...]
 
-    def store(at, count):
-        part = pl.ds(at, count)
-        pltpu.make_async_copy(r.out.at[part], r.out_hbm.at[part], r.store_sem).start()
-
-    total = pair_tile(r, slab_tile, columns, first, store)
+    total = pair_tile(r, slab_tile, columns, first)
     r.grads[pl.ds(0, columns), :] = total * r.live_column[...]
     gathered = nn(r.spread_rows[...], r.grads[...].astype(BF)).astype(BF)
     r.gmsg[...] = gathered.reshape(np_, 16, E)
     me.to_plane(lambda peer: r.gmsg.at[peer], r.gbuf, r.send_sem.at[5], r.recv_sem.at[5])
     r.gbuf[q] = r.gmsg[q]
+    pair_results(r, slab_tile, columns, first)
+    store = pltpu.make_async_copy(r.out, r.out_hbm, r.store_sem)
+    store.start()
     wait_bytes(r.gbuf, np_ - 1, r.recv_sem.at[5])
     by_column = jnp.sum(r.gbuf[...].astype(F32).reshape(pr, pc, 16, E), axis=0)
     over_columns = jnp.sum(by_column, axis=0)
@@ -518,7 +531,7 @@
     wait_bytes(r.hbuf, nz - 1, r.send_sem.at[6])
     wait_bytes(r.fbuf, np_ - 1, r.recv_sem.at[7])
     tiles = r.fbuf[...].reshape(8 * np_, E).astype(BF)
-    pltpu.make_async_copy(r.out, r.out_hbm, r.store_sem).wait()
+    store.wait()
     left = nn(left_pick, tiles).astype(BF)
     right = nn(right_pick, tiles).astype(BF)
     r.lm[...] = (nt(r.pp[:, :E], left) + nt(r.pp[:, E:], right)).astype(BF)
@@ -555,7 +568,9 @@
         "chain": vmem(chain.shape, jnp.int32),
         "mask_flat": pltpu.SMEM(mask_flat.shape, jnp.int32),
         "chain_flat": pltpu.SMEM(chain_flat.shape, jnp.int32),
-        "scores": vmem((nz, rb, rb), F32),
+        "scores": vmem((nz, 8 * np_, rb), F32),
+        "q_twice": vmem((8 * np_, E), BF),
+        "weights": vmem((steps, 8 * np_, 2 * rb), BF),
         "perm": vmem((8 * np_, rb), BF),
         "pick": vmem((pc * 16, 8 * nz), BF),
         "place_rows": vmem((columns + tile, 16 * np_), BF),
@@ -581,6 +596,7 @@
         "live_column": vmem((columns, E), F32),
         "chain_column": vmem((columns, E), F32),
         "right_live": vmem((columns, E), F32),
+        "act": vmem(cot.shape[:2] + w_in.shape[1:], BF),
         "d_act": vmem(cot.shape[:2] + w_in.shape[1:], D_ACT),
         "grads": vmem((columns + tile, E), F32),
         "gmsg": vmem((np_, 16, E), BF),

time: 81.1 us -> 80.4 us (level)
  no operation moved by 1% of the time
where the time goes in v6:
time: 80.4 us; the launch traced here: 80.3 us
  Pallas kernels  79 us (98%)
  between operations  1.29 us (2%)
    pallas_call x1, Pallas kernels, fused(): pl.pallas_call(functools.partial(kernel, sizes, INPUTS + ('out_hbm', 'lm'...  76.9 us
    pallas_call x1, Pallas kernels, store(): pl.pallas_call(store_kernel, out_shape=tuple((jax.ShapeDtypeStruct(a.shap...  2.12 us

profile of v6, /device:TPU:1, one launch (start us, length us, event | category | flops | bytes accessed | tf_op | source)
XLA Modules:
  0.0 80.3 jit_solution(1095789822113133298)
XLA Ops:
  1.3 76.9 %attend_pair_and_gradient.1 = (bf16[16,256,128]{2,1,0:T(8,128)(2,1)}, bf16[160,128]{1,0:T(8,128)(2,1)}) custom-call(s32[1]{0:T(128)S(6)} %copy.16.refs_0_, bf16[128,128]{1,0:T(8,128)(2,1)} %refs_1_.1, bf16[128,128]{1,0:T(8,128)(2,1)} %refs_2_.1, bf16[128,128]{1,0:T(8,128)(2,1)} %refs_3_.1, bf16[160,128]{1,0:T(8,128)(2,1)} %bitcast.5, ...), custom_call_target="tpu_custom_call" | custom-call | tf_op jit(solution)/shard_map/attend_pair_and_gradient/pallas_call | solution.py:615
  78.2 2.1 %store_results.1 = (bf16[16,256,128]{2,1,0:T(8,128)(2,1)}, bf16[160,128]{1,0:T(8,128)(2,1)}) custom-call(bf16[16,256,128]{2,1,0:T(8,128)(2,1)} %get-tuple-element.6.out, bf16[160,128]{1,0:T(8,128)(2,1)} %get-tuple-element.7.lm), custom_call_target="tpu_custom_call" | custom-call | tf_op jit(solution)/shard_map/store_results/pallas_call | solution.py:651

commit v7 on v6

--- a/solution.py
+++ b/solution.py
@@ -37,16 +37,27 @@
     return n.bit_length() - 1
 
 
+def plane_hops(pr, pc, m):
+    if (pr, pc) != (4, 8):
+        return 1
+    ring = (0, 1, 2, 1)
+    return ring[(m >> 1) & 3] + ring[((m & 1) << 1) | (m >> 4)]
+
+
 def plane_order(pr, pc):
-    offsets = list(range(1, pr * pc))
-    if (pr, pc) != (4, 8):
-        return offsets
-    ring = (0, 1, 2, 1)
-
-    def hops(m):
-        return ring[(m >> 1) & 3] + ring[((m & 1) << 1) | (m >> 4)]
-
-    return sorted(offsets, key=lambda m: -hops(m))
+    return sorted(range(1, pr * pc), key=lambda m: -plane_hops(pr, pc, m))
+
+
+def plane_greeted(pr, pc):
+    return [m for m in plane_order(pr, pc) if plane_hops(pr, pc, m) <= 2]
+
+
+def plane_witnesses(pr, pc):
+    witnesses = [1, 4] if (pr, pc) == (4, 8) else []
+    greeted = plane_greeted(pr, pc)
+    for m in range(1, pr * pc):
+        assert any(m ^ w in greeted or m == w for w in [0] + witnesses)
+    return witnesses
 
 
 def group_of(nz):
@@ -76,13 +87,12 @@
         return peer, (peer, self.prow, self.pcol)
 
     def near(self):
-        reach = max(2, group_of(self.nz) // 2)
-        return sorted({way * d % self.nz for d in range(1, reach + 1) for way in (1, -1)} - {0})
+        return sorted({way * d % self.nz for d in (1, 2) for way in (1, -1)} - {0})
 
     def greeted(self):
         for i in self.near():
             yield self.z_peer(i)[1]
-        for m in plane_order(self.pr, self.pc):
+        for m in plane_greeted(self.pr, self.pc):
             yield self.plane_peer(m)[1]
 
     def signal_all(self, barrier):
@@ -90,7 +100,7 @@
             pl.semaphore_signal(barrier, inc=1, device_id=device, device_id_type=MESH)
 
     def wait_all(self, barrier):
-        pl.semaphore_wait(barrier, self.np - 1 + len(self.near()))
+        pl.semaphore_wait(barrier, len(plane_greeted(self.pr, self.pc)) + len(self.near()))
 
     def send(self, source, target, send_sem, recv_sem, device):
         pltpu.make_async_remote_copy(
@@ -243,9 +253,9 @@
     return total
 
 
-def pair_results(r, tile, columns, first):
+def pair_results(r, rows, columns, first):
     right = r.ab[pl.ds(0, columns), :]
-    for t in range(tile):
+    for t in rows:
         same = r.chain_column[...] == r.chain_flat[first + t].astype(F32)
         live = r.mask_flat[first + t].astype(F32)
         seed = r.ab[pl.ds(columns + t, 1), :] * right + jnp.where(
@@ -308,6 +318,12 @@
     for chain in range(4):
         pass_on(chain, 0)
 
+    witnesses = plane_witnesses(pr, pc)
+    for m in witnesses:
+        pl.semaphore_signal(
+            r.known_sem, inc=1, device_id=me.plane_peer(m)[1], device_id_type=MESH
+        )
+
     loads["pp"].wait()
     row, column = grid_of(wz, W)
     piece = nt(one_hot(column == row + lax.rem(z, group) * wz), r.pp[...]).astype(BF)
@@ -315,7 +331,6 @@
     piece = nn(piece, one_hot(column == row + ((fd * q) & 127))).astype(BF)
     r.ppmsg[...] = piece
     r.ppg[q] = piece
-    me.to_plane(lambda peer: r.ppmsg, r.ppg, r.send_sem.at[0], r.recv_sem.at[0])
 
     row, column = grid_of(8 * np_, rb)
     r.perm[...] = one_hot(column == (row & 3) * np_ + (row >> 3))
@@ -337,6 +352,9 @@
         r.scores[block] = jnp.where(live > 0, raw, -1e30)
 
     score(z)
+    if witnesses:
+        pl.semaphore_wait(r.known_sem, len(witnesses))
+    me.to_plane(lambda peer: r.ppmsg, r.ppg, r.send_sem.at[0], r.recv_sem.at[0])
 
     def arrive(chain, distance):
         if distance <= furthest[chain]:
@@ -427,13 +445,13 @@
     for distance in range(2, last, 2):
         for chain in range(4):
             arrive(chain, distance)
-        for chore in chores.pop(distance, ()):
-            chore()
         for near in (distance - 1, distance):
             if near % 2:
                 for chain in range(2):
                     arrive(chain, near)
             score_at(near)
+        for chore in chores.pop(distance, ()):
+            chore()
     for stage in (2, 4, 6):
         for chore in chores.pop(stage, ()):
             chore()
@@ -494,9 +512,8 @@
     r.gmsg[...] = gathered.reshape(np_, 16, E)
     me.to_plane(lambda peer: r.gmsg.at[peer], r.gbuf, r.send_sem.at[5], r.recv_sem.at[5])
     r.gbuf[q] = r.gmsg[q]
-    pair_results(r, slab_tile, columns, first)
-    store = pltpu.make_async_copy(r.out, r.out_hbm, r.store_sem)
-    store.start()
+    split = slab_tile * 3 // 8
+    pair_results(r, range(split), columns, first)
     wait_bytes(r.gbuf, np_ - 1, r.recv_sem.at[5])
     by_column = jnp.sum(r.gbuf[...].astype(F32).reshape(pr, pc, 16, E), axis=0)
     over_columns = jnp.sum(by_column, axis=0)
@@ -509,6 +526,9 @@
         r.zmsg[other] = jnp.where((sub >> 2) == other % 2, by_column[other // 2, 0:8, :], lefts)
     me.to_column(lambda peer: r.zmsg.at[peer], r.hbuf, r.send_sem.at[6], r.recv_sem.at[6])
     r.hbuf[z] = r.zmsg[z]
+    pair_results(r, range(split, slab_tile), columns, first)
+    store = pltpu.make_async_copy(r.out, r.out_hbm, r.store_sem)
+    store.start()
     wait_bytes(r.hbuf, nz - 1, r.recv_sem.at[6])
     tile = jnp.sum(r.hbuf[...], axis=0).astype(BF).astype(F32)
     r.fmsg[...] = tile
@@ -605,6 +625,7 @@
         "hbuf": vmem((nz, 8, E), F32),
         "fmsg": vmem((8, E), F32),
         "fbuf": vmem((np_, 8, E), F32),
+        "known_sem": pltpu.SemaphoreType.REGULAR,
         "load_sem": dma((len(LOADS),)),
         "ring_send": dma((4, steps)),
         "ring_recv": dma((4, steps)),

time: 80.4 us -> 80 us (level)
  no operation moved by 1% of the time
where the time goes in v7:
time: 80 us; the launch traced here: 79.8 us
  Pallas kernels  78.5 us (98%)
  between operations  1.29 us (2%)
    pallas_call x1, Pallas kernels, fused(): pl.pallas_call(functools.partial(kernel, sizes, INPUTS + ('out_hbm', 'lm'...  76.4 us
    pallas_call x1, Pallas kernels, store(): pl.pallas_call(store_kernel, out_shape=tuple((jax.ShapeDtypeStruct(a.shap...  2.12 us

profile of v7, /device:TPU:1, one launch (start us, length us, event | category | flops | bytes accessed | tf_op | source)
XLA Modules:
  0.0 79.8 jit_solution(8755923360583261504)
XLA Ops:
  1.3 76.4 %attend_pair_and_gradient.1 = (bf16[16,256,128]{2,1,0:T(8,128)(2,1)}, bf16[160,128]{1,0:T(8,128)(2,1)}) custom-call(s32[1]{0:T(128)S(6)} %copy.16.refs_0_, bf16[128,128]{1,0:T(8,128)(2,1)} %refs_1_.1, bf16[128,128]{1,0:T(8,128)(2,1)} %refs_2_.1, bf16[128,128]{1,0:T(8,128)(2,1)} %refs_3_.1, bf16[160,128]{1,0:T(8,128)(2,1)} %bitcast.5, ...), custom_call_target="tpu_custom_call" | custom-call | tf_op jit(solution)/shard_map/attend_pair_and_gradient/pallas_call | solution.py:636
  77.7 2.1 %store_results.1 = (bf16[16,256,128]{2,1,0:T(8,128)(2,1)}, bf16[160,128]{1,0:T(8,128)(2,1)}) custom-call(bf16[16,256,128]{2,1,0:T(8,128)(2,1)} %get-tuple-element.6.out, bf16[160,128]{1,0:T(8,128)(2,1)} %get-tuple-element.7.lm), custom_call_target="tpu_custom_call" | custom-call | tf_op jit(solution)/shard_map/store_results/pallas_call | solution.py:672

commit v8 on v7

--- a/solution.py
+++ b/solution.py
@@ -433,12 +433,12 @@
             r.d_act[t] = nt(r.cot[t], r.w_out_half[...]).astype(r.d_act.dtype)
 
     last = nz // 2
-    third = max(1, slab_tile // 4)
+    half_tile = slab_tile // 2
     chores = {
         0: (make_pair_constants, make_picks),
-        2: (lambda: loads["cot"].wait(), lambda: make_d_act(0, third)),
+        2: (lambda: loads["cot"].wait(), lambda: make_d_act(0, half_tile)),
         4: (make_w2,),
-        6: (lambda: make_d_act(third, slab_tile),),
+        6: (lambda: make_d_act(half_tile, slab_tile),),
     }
     for chore in chores[0]:
         chore()
@@ -455,34 +455,48 @@
     for stage in (2, 4, 6):
         for chore in chores.pop(stage, ()):
             chore()
+
+    def blocks_at(distance):
+        left = lax.rem(z - distance + nz, nz)
+        if distance in (0, last):
+            return [left]
+        return [left, lax.rem(z + distance, nz)]
+
+    def attend(distances):
+        blocks = [b for distance in distances for b in blocks_at(distance)]
+        top = r.scores[blocks[0]]
+        for b in blocks[1:]:
+            top = jnp.maximum(top, r.scores[b])
+        top = jnp.max(top, axis=1, keepdims=True)
+        pairs = [blocks[i : i + 2] for i in range(0, len(blocks), 2)]
+        below = jnp.zeros((8 * np_, rb), F32)
+        weights = []
+        for pair in pairs:
+            shifted = [jnp.exp(r.scores[b] - top) for b in pair]
+            for part in shifted:
+                below = below + part
+            weights.append(jnp.concatenate(shifted, axis=1).astype(BF))
+        below = jnp.sum(below, axis=1, keepdims=True)
+        for distance in distances:
+            if distance % 2 or distance == last:
+                for chain in (2, 3):
+                    arrive(chain, distance)
+        above = jnp.zeros((8 * np_, E), F32)
+        for pair, weight in zip(pairs, weights):
+            above = above + nn(weight, jnp.concatenate([r.v[b] for b in pair], axis=0))
+        return top, below, above
+
+    top, below, above = attend(range(last - 1))
     for chain in (0, 1):
         arrive(chain, last)
         arrive(chain, last - 1)
     score_at(last - 1)
     score_at(last)
-
-    top = r.scores[0]
-    for b in range(1, nz):
-        top = jnp.maximum(top, r.scores[b])
-    top = jnp.max(top, axis=1, keepdims=True)
-    def pair_of(distance):
-        left = lax.rem(z - distance + nz, nz)
-        return left, lax.rem(z + (distance if distance < last else 0), nz)
-
-    below = jnp.zeros((8 * np_, rb), F32)
-    for distance in range(1, last + 1):
-        shifted = [jnp.exp(r.scores[b] - top) for b in pair_of(distance)]
-        below = below + shifted[0] + shifted[1]
-        r.weights[distance - 1] = jnp.concatenate(shifted, axis=1).astype(BF)
-    below = 1.0 / jnp.sum(below, axis=1, keepdims=True)
-    above = jnp.zeros((8 * np_, E), F32)
-    for distance in range(1, last + 1):
-        if distance % 2 or distance == last:
-            for chain in (2, 3):
-                arrive(chain, distance)
-        both = jnp.concatenate([r.v[b] for b in pair_of(distance)], axis=0)
-        above = above + nn(r.weights[distance - 1], both)
-    attended = (above * below).astype(BF)
+    top_late, below_late, above_late = attend((last, last - 1))
+    highest = jnp.maximum(top, top_late)
+    early, late = jnp.exp(top - highest), jnp.exp(top_late - highest)
+    below = 1.0 / (below * early + below_late * late)
+    attended = ((above * early + above_late * late) * below).astype(BF)
     wait_bytes(r.w2g, group - 1, r.recv_sem.at[1])
     both = nt(attended, r.w2g[...].reshape(W, E))
     terms = jnp.where(is_left, both[:, :E], both[:, E:]) + r.presidual[...]
@@ -535,10 +549,10 @@
     r.fbuf[q] = tile
     me.to_plane(lambda peer: r.fmsg, r.fbuf, r.send_sem.at[7], r.recv_sem.at[7])
     odd = z & 1
-    row, column = grid_of(rb, 8 * np_)
-    base = (row & (np_ - 1)) * 8 + (row >> log_np)
-    left_pick = one_hot(column == base + 4 * (1 - odd))
-    right_pick = one_hot(column == base + 4 * odd)
+    row, column = grid_of(2 * rb, 8 * np_)
+    half = jnp.where(row < rb, 1 - odd, odd)
+    base = (row & (np_ - 1)) * 8 + ((row >> log_np) & 3)
+    halves = one_hot(column == base + 4 * half)
     for chain in range(4):
         for distance in range(1, furthest[chain] + 1):
             ring(chain, distance, 1 if distance % 2 else 2).wait_send()
@@ -552,9 +566,9 @@
     wait_bytes(r.fbuf, np_ - 1, r.recv_sem.at[7])
     tiles = r.fbuf[...].reshape(8 * np_, E).astype(BF)
     store.wait()
-    left = nn(left_pick, tiles).astype(BF)
-    right = nn(right_pick, tiles).astype(BF)
-    r.lm[...] = (nt(r.pp[:, :E], left) + nt(r.pp[:, E:], right)).astype(BF)
+    halves = nn(halves, tiles).astype(BF)
+    halves = jnp.concatenate([halves[:rb], halves[rb:]], axis=1)
+    r.lm[...] = nt(r.pp[...], halves).astype(BF)
     wait_bytes(r.fbuf, np_ - 1, r.send_sem.at[7])
 
 
@@ -590,7 +604,6 @@
         "chain_flat": pltpu.SMEM(chain_flat.shape, jnp.int32),
         "scores": vmem((nz, 8 * np_, rb), F32),
         "q_twice": vmem((8 * np_, E), BF),
-        "weights": vmem((steps, 8 * np_, 2 * rb), BF),
         "perm": vmem((8 * np_, rb), BF),
         "pick": vmem((pc * 16, 8 * nz), BF),
         "place_rows": vmem((columns + tile, 16 * np_), BF),

time: 80 us -> 80.3 us (level)
  no operation moved by 1% of the time
where the time goes in v8:
time: 80.3 us; the launch traced here: 80.1 us
  Pallas kernels  78.8 us (98%)
  between operations  1.29 us (2%)
    pallas_call x1, Pallas kernels, fused(): pl.pallas_call(functools.partial(kernel, sizes, INPUTS + ('out_hbm', 'lm'...  76.7 us
    pallas_call x1, Pallas kernels, store(): pl.pallas_call(store_kernel, out_shape=tuple((jax.ShapeDtypeStruct(a.shap...  2.12 us

profile of v8, /device:TPU:1, one launch (start us, length us, event | category | flops | bytes accessed | tf_op | source)
XLA Modules:
  0.0 80.1 jit_solution(14323155569501666714)
XLA Ops:
  1.3 76.7 %attend_pair_and_gradient.1 = (bf16[16,256,128]{2,1,0:T(8,128)(2,1)}, bf16[160,128]{1,0:T(8,128)(2,1)}) custom-call(s32[1]{0:T(128)S(6)} %copy.16.refs_0_, bf16[128,128]{1,0:T(8,128)(2,1)} %refs_1_.1, bf16[128,128]{1,0:T(8,128)(2,1)} %refs_2_.1, bf16[128,128]{1,0:T(8,128)(2,1)} %refs_3_.1, bf16[160,128]{1,0:T(8,128)(2,1)} %bitcast.5, ...), custom_call_target="tpu_custom_call" | custom-call | tf_op jit(solution)/shard_map/attend_pair_and_gradient/pallas_call | solution.py:649
  78.0 2.1 %store_results.1 = (bf16[16,256,128]{2,1,0:T(8,128)(2,1)}, bf16[160,128]{1,0:T(8,128)(2,1)}) custom-call(bf16[16,256,128]{2,1,0:T(8,128)(2,1)} %get-tuple-element.6.out, bf16[160,128]{1,0:T(8,128)(2,1)} %get-tuple-element.7.lm), custom_call_target="tpu_custom_call" | custom-call | tf_op jit(solution)/shard_map/store_results/pallas_call | solution.py:685

commit v9 on v8

--- a/solution.py
+++ b/solution.py
@@ -112,8 +112,8 @@
             device_id_type=MESH,
         ).start()
 
-    def to_plane(self, source, target, send_sem, recv_sem):
-        for m in plane_order(self.pr, self.pc):
+    def to_plane(self, source, target, send_sem, recv_sem, offsets=None):
+        for m in plane_order(self.pr, self.pc) if offsets is None else offsets:
             peer, device = self.plane_peer(m)
             self.send(source(peer), target.at[self.q], send_sem, recv_sem, device)
 
@@ -331,6 +331,12 @@
     piece = nn(piece, one_hot(column == row + ((fd * q) & 127))).astype(BF)
     r.ppmsg[...] = piece
     r.ppg[q] = piece
+    greeted = plane_greeted(pr, pc)
+
+    def share_piece(offsets):
+        me.to_plane(lambda peer: r.ppmsg, r.ppg, r.send_sem.at[0], r.recv_sem.at[0], offsets)
+
+    share_piece(greeted)
 
     row, column = grid_of(8 * np_, rb)
     r.perm[...] = one_hot(column == (row & 3) * np_ + (row >> 3))
@@ -354,7 +360,7 @@
     score(z)
     if witnesses:
         pl.semaphore_wait(r.known_sem, len(witnesses))
-    me.to_plane(lambda peer: r.ppmsg, r.ppg, r.send_sem.at[0], r.recv_sem.at[0])
+        share_piece([m for m in plane_order(pr, pc) if m not in greeted])
 
     def arrive(chain, distance):
         if distance <= furthest[chain]:

time: 80.3 us -> 79.7 us (level)
  no operation moved by 1% of the time
where the time goes in v9:
time: 79.7 us; the launch traced here: 79.6 us
  Pallas kernels  78.3 us (98%)
  between operations  1.29 us (2%)
    pallas_call x1, Pallas kernels, fused(): pl.pallas_call(functools.partial(kernel, sizes, INPUTS + ('out_hbm', 'lm'...  76.2 us
    pallas_call x1, Pallas kernels, store(): pl.pallas_call(store_kernel, out_shape=tuple((jax.ShapeDtypeStruct(a.shap...  2.12 us

profile of v9, /device:TPU:1, one launch (start us, length us, event | category | flops | bytes accessed | tf_op | source)
XLA Modules:
  0.0 79.6 jit_solution(9882888845195898073)
XLA Ops:
  1.3 76.2 %attend_pair_and_gradient.1 = (bf16[16,256,128]{2,1,0:T(8,128)(2,1)}, bf16[160,128]{1,0:T(8,128)(2,1)}) custom-call(s32[1]{0:T(128)S(6)} %copy.16.refs_0_, bf16[128,128]{1,0:T(8,128)(2,1)} %refs_1_.1, bf16[128,128]{1,0:T(8,128)(2,1)} %refs_2_.1, bf16[128,128]{1,0:T(8,128)(2,1)} %refs_3_.1, bf16[160,128]{1,0:T(8,128)(2,1)} %bitcast.5, ...), custom_call_target="tpu_custom_call" | custom-call | tf_op jit(solution)/shard_map/attend_pair_and_gradient/pallas_call | solution.py:655
  77.5 2.1 %store_results.1 = (bf16[16,256,128]{2,1,0:T(8,128)(2,1)}, bf16[160,128]{1,0:T(8,128)(2,1)}) custom-call(bf16[16,256,128]{2,1,0:T(8,128)(2,1)} %get-tuple-element.6.out, bf16[160,128]{1,0:T(8,128)(2,1)} %get-tuple-element.7.lm), custom_call_target="tpu_custom_call" | custom-call | tf_op jit(solution)/shard_map/store_results/pallas_call | solution.py:691
